TPU v7x, 256 devices: a whole 4x4x8 slice. The times are simulated.
256 devices in a mesh: dp: 8 (over z_hi, x), ctx: 32 (over z_lo, y, core).
Axes of the slice: x: 4, y: 4, z: 8 (z_hi: 2, z_lo: 4; z = z_hi * 4 + z_lo), core: 2. Of those that a mesh axis runs over, the one named last changes fastest.
Arguments:
- tokens: bfloat16 [8, 4096, 512], P('dp', 'ctx'), may hold values from -6 to 6
- cotangent: bfloat16 [8, 4096, 512], P('dp', 'ctx'), may hold values from -6 to 6
- decay: float32 [8, 512], replicated, may hold values from 0 to 1, as said below
- residue: float32 [8, 512], replicated, may hold values from -1 to 1
- skip: float32 [512], replicated, may hold values from -3 to 3
Outputs:
- grad_tokens: float32 [8, 4096, 512], P('dp', 'ctx')
- grad_residue: float32 [8, 512], P(None, 'ctx')
- grad_decay: float32 [8, 512], P(None, 'ctx')
- grad_skip: float32 [512], P('ctx')
Inputs may be any that keep to these rules, and one draw needn't show every extreme that they name: `decay`: positive.
All inputs are finite; a program needn't handle non-finite values.
Results may differ from a plain program's by a relative error of at most 0.0003.
Values may be sent and summed in bfloat16 or wider, within the bound.
A program may use at most 128 MiB of HBM per device.

v0:
```python
import jax
import jax.numpy as jnp
from jax import lax
from jax.sharding import PartitionSpec as P

BLOCK = 8


precise = lax.Precision.HIGHEST


def pair_combine(former, latter):
    return (former[0] * latter[0], latter[0] * former[1] + latter[1])


def local_pass(rows_in, rows_grad, decay, block_len):
    length, columns = rows_in.shape
    mode_count = decay.shape[0]
    nblocks = length // block_len
    block_in = rows_in.reshape(nblocks, block_len, columns)
    block_grad = rows_grad.reshape(nblocks, block_len, columns)
    offsets = jnp.arange(block_len, dtype=jnp.float32)
    offset = offsets[:, None] - offsets[None, :]
    inside = (offset > 0).astype(jnp.float32)
    lagged = jnp.maximum(offset - 1.0, 0.0)
    fprev_list = []
    gnext_list = []
    forward_list = []
    backward_list = []
    for mode in range(mode_count):
        rate = decay[mode]
        weights = inside[:, :, None] * jnp.exp(-rate[None, None, :] * lagged[:, :, None])
        fprev_in = jnp.einsum("bic,jic->bjc", block_in, weights, precision=precise)
        gnext_in = jnp.einsum("bic,ijc->bjc", block_grad, weights, precision=precise)
        factor = jnp.exp(-rate)
        block_ends = factor * fprev_in[:, -1] + block_in[:, -1]
        block_starts = factor * gnext_in[:, 0] + block_grad[:, 0]
        block_decay = jnp.broadcast_to(jnp.exp(-rate * block_len), block_ends.shape)
        forward_list.append(lax.associative_scan(pair_combine, (block_decay, block_ends))[1])
        backward_list.append(
            lax.associative_scan(pair_combine, (block_decay, block_starts), reverse=True)[1]
        )
        fprev_list.append(fprev_in)
        gnext_list.append(gnext_in)
    forward_sums = jnp.stack(forward_list, axis=0)
    backward_sums = jnp.stack(backward_list, axis=0)
    return (block_in, block_grad, fprev_list, gnext_list, forward_sums, backward_sums)


def finish(pieces, decay, residue, skip, start_state, end_state):
    block_in, block_grad, fprev_list, gnext_list, forward_sums, backward_sums = pieces
    nblocks, block_len, columns = block_in.shape
    mode_count = decay.shape[0]
    block_index = jnp.arange(nblocks, dtype=jnp.float32)[:, None]
    offsets = jnp.arange(block_len, dtype=jnp.float32)[:, None]
    zeros_row = jnp.zeros((1, columns), jnp.float32)
    sum_skip = jnp.sum(block_grad * block_in, axis=(0, 1))
    grads_rows = skip * block_grad
    residue_rows = []
    decay_rows = []
    for mode in range(mode_count):
        rate = decay[mode]
        factor = jnp.exp(-rate)
        fcarry = (
            jnp.concatenate([zeros_row, forward_sums[mode, :-1]], axis=0)
            + jnp.exp(-rate * block_len * block_index) * start_state[mode]
        )
        gcarry = (
            jnp.concatenate([backward_sums[mode, 1:], zeros_row], axis=0)
            + jnp.exp(-rate * block_len * (nblocks - 1 - block_index)) * end_state[mode]
        )
        fprev = fprev_list[mode] + jnp.exp(-rate * offsets)[None] * fcarry[:, None]
        gnow = (
            factor
            * (
                gnext_list[mode]
                + jnp.exp(-rate * (block_len - 1 - offsets))[None] * gcarry[:, None]
            )
            + block_grad
        )
        grads_rows = grads_rows + residue[mode] * gnow
        residue_rows.append(factor * jnp.sum(block_grad * fprev, axis=(0, 1)) + sum_skip)
        decay_rows.append(jnp.sum(gnow * fprev, axis=(0, 1)))
    partial_value = jnp.stack(residue_rows + decay_rows + [sum_skip], axis=0)
    return (grads_rows.reshape(nblocks * block_len, columns), partial_value)


def body(tokens, cotangent, decay, residue, skip):
    block_len = BLOCK
    length = tokens.shape[1]
    channels = tokens.shape[2]
    mode_count = decay.shape[0]
    shards = lax.axis_size("ctx")
    narrow = channels // shards
    column_start = lax.axis_index("ctx") * narrow
    own_decay = lax.dynamic_slice_in_dim(decay, column_start, narrow, 1)
    own_residue = lax.dynamic_slice_in_dim(residue, column_start, narrow, 1)
    own_skip = lax.dynamic_slice_in_dim(skip, column_start, narrow, 0)
    moved_in, moved_grad = (
        lax.all_to_all(
            tokens[0].reshape(length, 1, channels), "ctx", split_axis=2, concat_axis=1, tiled=True
        ),
        lax.all_to_all(
            cotangent[0].reshape(length, 1, channels),
            "ctx",
            split_axis=2,
            concat_axis=1,
            tiled=True,
        ),
    )
    segment_in = moved_in.reshape(length, shards * narrow).astype(jnp.float32)
    segment_grad = moved_grad.reshape(length, shards * narrow).astype(jnp.float32)
    wide_decay = jnp.tile(own_decay, (1, shards))
    wide_residue = jnp.tile(own_residue, (1, shards))
    wide_skip = jnp.tile(own_skip, (shards,))
    pieces = local_pass(segment_in, segment_grad, wide_decay, block_len)
    start_sum = pieces[4][:, -1].reshape(mode_count, shards, narrow)
    end_sum = pieces[5][:, 0].reshape(mode_count, shards, narrow)
    segment_decay = jnp.broadcast_to(jnp.exp(-own_decay * length)[:, None, :], start_sum.shape)
    forward_totals = lax.associative_scan(pair_combine, (segment_decay, start_sum), axis=1)[1]
    backward_totals = lax.associative_scan(
        pair_combine, (segment_decay, end_sum), reverse=True, axis=1
    )[1]
    zeros_column = jnp.zeros((mode_count, 1, narrow), jnp.float32)
    start_state = jnp.concatenate([zeros_column, forward_totals[:, :-1]], axis=1).reshape(
        mode_count, shards * narrow
    )
    end_state = jnp.concatenate([backward_totals[:, 1:], zeros_column], axis=1).reshape(
        mode_count, shards * narrow
    )
    grads_rows, partial_value = finish(
        pieces, wide_decay, wide_residue, wide_skip, start_state, end_state
    )
    returned = lax.all_to_all(
        grads_rows.reshape(length, shards, narrow), "ctx", split_axis=1, concat_axis=2, tiled=True
    )
    grad_tokens = returned.reshape(1, length, channels)
    partial_value = partial_value.reshape(2 * mode_count + 1, shards, narrow).sum(axis=1)
    totals = lax.psum(partial_value, "dp")
    token_total = length * shards * lax.axis_size("dp")
    grad_residue = totals[:mode_count] / token_total
    grad_decay = (
        -jnp.exp(-own_decay) * own_residue * totals[mode_count : 2 * mode_count] / token_total
    )
    grad_skip = totals[2 * mode_count] / token_total
    return (grad_tokens, grad_residue, grad_decay, grad_skip)


def solution(mesh):
    return jax.shard_map(
        body,
        mesh=mesh,
        in_specs=(P("dp", "ctx", None), P("dp", "ctx", None), P(), P(), P()),
        out_specs=(P("dp", "ctx", None), P(None, "ctx"), P(None, "ctx"), P("ctx")),
        check_vma=False,
    )
```

profile of v0, /device:TPU:1, one launch (start us, length us, event | category | flops | bytes accessed | tf_op | source)
XLA Modules:
  0.0 328.1 jit_solution(7991080120659416163)
XLA Ops:
  4.3 10.2 %all-to-all-start.2 = ((bf16[32,2,1024]{2,1,0:T(2,128)(2,1)}), bf16[32,2,1024]{2,1,0:T(2,128)(2,1)S(1)}, u32[]{:S(2)}, u32[]{:S(2)}) async-start(bf16[32,2,1024]{2,1,0:T(2,128)(2,1)} %reshape.1714), calls=%async_computation.2 | async-start | bytes 262144 | tf_op jit(solution)/shard_map/all_to_all | solution.py:100
  52.9 8.4 %all-to-all-start = ((bf16[32,2,1024]{2,1,0:T(2,128)(2,1)}), bf16[32,2,1024]{2,1,0:T(2,128)(2,1)S(1)}, u32[]{:S(2)}, u32[]{:S(2)}) async-start(bf16[32,2,1024]{2,1,0:T(2,128)(2,1)} %reshape.1712), calls=%async_computation | async-start | bytes 262144 | tf_op jit(solution)/shard_map/all_to_all | solution.py:103
  63.1 3.9 %fusion = f32[512,8,16]{2,1,0:T(8,128)} fusion(bf16[16,8,512]{0,1,2:T(8,128)(2,1)S(1)} %copy.1035, f32[512]{0:T(512)S(1)} %neg.430, f32[8,8]{1,0:T(8,128)S(1)} %add_maximum_fusion, f32[8,8]{1,0:T(8,128)S(1)} %fusion.133), kind=kOutput, calls=%fused_computation.1 | convolution fusion | flops 6356992 | bytes 395776 | tf_op jit(solution)/shard_map/bic,jic->bjc/dot_general | solution.py:33
  67.0 3.9 %fusion.2 = f32[512,8,16]{2,1,0:T(8,128)} fusion(bf16[16,8,512]{0,1,2:T(8,128)(2,1)S(1)} %copy.1035, f32[512]{0:T(512)S(1)} %neg.427, f32[8,8]{1,0:T(8,128)S(1)} %add_maximum_fusion, f32[8,8]{1,0:T(8,128)S(1)} %fusion.133), kind=kOutput, calls=%fused_computation.4 | convolution fusion | flops 6356992 | bytes 395776 | tf_op jit(solution)/shard_map/bic,jic->bjc/dot_general | solution.py:33
  70.9 3.9 %fusion.10 = f32[512,8,16]{2,1,0:T(8,128)} fusion(bf16[16,8,512]{0,1,2:T(8,128)(2,1)S(1)} %copy.1035, f32[512]{0:T(512)S(1)} %neg.415, f32[8,8]{1,0:T(8,128)S(1)} %add_maximum_fusion, f32[8,8]{1,0:T(8,128)S(1)} %fusion.133), kind=kOutput, calls=%fused_computation.16 | convolution fusion | flops 6356992 | bytes 395776 | tf_op jit(solution)/shard_map/bic,jic->bjc/dot_general | solution.py:33
  74.8 3.9 %fusion.8 = f32[512,8,16]{2,1,0:T(8,128)} fusion(bf16[16,8,512]{0,1,2:T(8,128)(2,1)S(1)} %copy.1035, f32[512]{0:T(512)S(1)} %neg.418, f32[8,8]{1,0:T(8,128)S(1)} %add_maximum_fusion, f32[8,8]{1,0:T(8,128)S(1)} %fusion.133), kind=kOutput, calls=%fused_computation.13 | convolution fusion | flops 6356992 | bytes 395776 | tf_op jit(solution)/shard_map/bic,jic->bjc/dot_general | solution.py:33
  78.7 3.9 %fusion.6 = f32[512,8,16]{2,1,0:T(8,128)} fusion(bf16[16,8,512]{0,1,2:T(8,128)(2,1)S(1)} %copy.1035, f32[512]{0:T(512)S(1)} %neg.421, f32[8,8]{1,0:T(8,128)S(1)} %add_maximum_fusion, f32[8,8]{1,0:T(8,128)S(1)} %fusion.133), kind=kOutput, calls=%fused_computation.10 | convolution fusion | flops 6356992 | bytes 395776 | tf_op jit(solution)/shard_map/bic,jic->bjc/dot_general | solution.py:33
  82.6 3.9 %fusion.4 = f32[512,8,16]{2,1,0:T(8,128)} fusion(bf16[16,8,512]{0,1,2:T(8,128)(2,1)S(1)} %copy.1035, f32[512]{0:T(512)S(1)} %neg.424, f32[8,8]{1,0:T(8,128)S(1)} %add_maximum_fusion, f32[8,8]{1,0:T(8,128)S(1)} %fusion.133), kind=kOutput, calls=%fused_computation.7 | convolution fusion | flops 6356992 | bytes 395776 | tf_op jit(solution)/shard_map/bic,jic->bjc/dot_general | solution.py:33
  86.5 4.1 %fusion.12 = f32[512,8,16]{2,1,0:T(8,128)} fusion(bf16[16,8,512]{0,1,2:T(8,128)(2,1)S(1)} %copy.1035, f32[512]{0:T(512)S(1)} %neg.412, f32[8,8]{1,0:T(8,128)S(1)} %add_maximum_fusion, f32[8,8]{1,0:T(8,128)S(1)} %fusion.133), kind=kOutput, calls=%fused_computation.19 | convolution fusion | flops 6356992 | bytes 395776 | tf_op jit(solution)/shard_map/bic,jic->bjc/dot_general | solution.py:33
  95.5 4.8 %fusion.3 = f32[512,8,16]{2,1,0:T(8,128)} fusion(bf16[16,8,512]{0,1,2:T(8,128)(2,1)S(1)} %copy.991, f32[512]{0:T(512)} %copy-done.92, f32[8,8]{1,0:T(8,128)S(1)} %add_maximum_fusion, f32[8,8]{1,0:T(8,128)S(1)} %fusion.133), kind=kOutput, calls=%fused_computation.5 | convolution fusion | flops 6356992 | bytes 395776 | tf_op jit(solution)/shard_map/bic,ijc->bjc/dot_general | solution.py:34
  100.3 4.2 %fusion.15 = f32[512,8,16]{2,1,0:T(8,128)} fusion(bf16[16,8,512]{0,1,2:T(8,128)(2,1)S(1)} %copy.991, f32[8,8]{1,0:T(8,128)S(1)} %add_maximum_fusion, f32[512]{0:T(512)S(1)} %copy-done.96, f32[8,8]{1,0:T(8,128)S(1)} %fusion.133), kind=kOutput, calls=%fused_computation.23 | convolution fusion | flops 6356992 | bytes 395776 | tf_op jit(solution)/shard_map/bic,ijc->bjc/dot_general | solution.py:34
  104.4 2.9 copy.1051
  109.0 2.9 copy.1049
  114.7 2.9 copy.1043
  117.6 3.3 copy.1045
  141.6 3.4 %fusion.1 = f32[512,8,16]{2,1,0:T(8,128)S(1)} fusion(bf16[16,8,512]{0,1,2:T(8,128)(2,1)S(1)} %copy.991, f32[512]{0:T(512)} %copy-done.93, f32[8,8]{1,0:T(8,128)S(1)} %add_maximum_fusion, f32[8,8]{1,0:T(8,128)S(1)} %fusion.133), kind=kOutput, calls=%fused_computation.2 | convolution fusion | flops 6356992 | bytes 395776 | tf_op jit(solution)/shard_map/bic,ijc->bjc/dot_general | solution.py:34
  145.0 4.8 %fusion.13 = f32[512,8,16]{2,1,0:T(8,128)} fusion(bf16[16,8,512]{0,1,2:T(8,128)(2,1)S(1)} %copy.991, f32[512]{0:T(512)} %copy-done.87, f32[8,8]{1,0:T(8,128)S(1)} %add_maximum_fusion, f32[8,8]{1,0:T(8,128)S(1)} %fusion.133), kind=kOutput, calls=%fused_computation.20 | convolution fusion | flops 6356992 | bytes 395776 | tf_op jit(solution)/shard_map/bic,ijc->bjc/dot_general | solution.py:34
  149.8 4.1 %fusion.11 = f32[512,8,16]{2,1,0:T(8,128)} fusion(bf16[16,8,512]{0,1,2:T(8,128)(2,1)S(1)} %copy.991, f32[512]{0:T(512)S(1)} %copy-done.86, f32[8,8]{1,0:T(8,128)S(1)} %add_maximum_fusion, f32[8,8]{1,0:T(8,128)S(1)} %fusion.133), kind=kOutput, calls=%fused_computation.17 | convolution fusion | flops 6356992 | bytes 395776 | tf_op jit(solution)/shard_map/bic,ijc->bjc/dot_general | solution.py:34
  153.9 4.2 %fusion.9 = f32[512,8,16]{2,1,0:T(8,128)} fusion(bf16[16,8,512]{0,1,2:T(8,128)(2,1)S(1)} %copy.991, f32[512]{0:T(512)S(1)} %copy-done.89, f32[8,8]{1,0:T(8,128)S(1)} %add_maximum_fusion, f32[8,8]{1,0:T(8,128)S(1)} %fusion.133), kind=kOutput, calls=%fused_computation.14 | convolution fusion | flops 6356992 | bytes 395776 | tf_op jit(solution)/shard_map/bic,ijc->bjc/dot_general | solution.py:34
  158.1 4.3 %fusion.7 = f32[512,8,16]{2,1,0:T(8,128)} fusion(bf16[16,8,512]{0,1,2:T(8,128)(2,1)S(1)} %copy.991, f32[512]{0:T(512)S(1)} %copy-done.91, f32[8,8]{1,0:T(8,128)S(1)} %add_maximum_fusion, f32[8,8]{1,0:T(8,128)S(1)} %fusion.133), kind=kOutput, calls=%fused_computation.11 | convolution fusion | flops 6356992 | bytes 395776 | tf_op jit(solution)/shard_map/bic,ijc->bjc/dot_general | solution.py:34
  162.3 4.2 %fusion.5 = f32[512,8,16]{2,1,0:T(8,128)} fusion(bf16[16,8,512]{0,1,2:T(8,128)(2,1)S(1)} %copy.991, f32[512]{0:T(512)S(1)} %copy-done.84, f32[8,8]{1,0:T(8,128)S(1)} %add_maximum_fusion, f32[8,8]{1,0:T(8,128)S(1)} %fusion.133), kind=kOutput, calls=%fused_computation.8 | convolution fusion | flops 6356992 | bytes 395776 | tf_op jit(solution)/shard_map/bic,ijc->bjc/dot_general | solution.py:34
  243.6 45.9 %psum.7 = f32[17,16]{1,0:T(8,128)S(1)} all-reduce(f32[17,16]{1,0:T(8,128)S(1)} %reduce_sum.206), channel_id=1, replica_groups=mesh['dp'=8,'ctx'=32] {'dp'}, use_global_device_ids=true, to_apply=%region_18.0 | all-reduce | flops 272 | bytes 2176 | tf_op jit(solution)/shard_map/psum | solution.py:139
  300.8 15.0 %all-to-all-start.1 = ((f32[128,32,16]{0,2,1:T(8,128)}), f32[128,32,16]{0,2,1:T(8,128)S(1)}, u32[]{:S(2)}, u32[]{:S(2)}) async-start(f32[128,32,16]{0,2,1:T(8,128)} %copy.1032), calls=%async_computation.1 | async-start | bytes 524288 | tf_op jit(solution)/shard_map/all_to_all | solution.py:134
  317.0 9.9 %all-to-all-done.1 = f32[128,32,16]{0,2,1:T(8,128)S(1)} async-done(((f32[128,32,16]{0,2,1:T(8,128)}), f32[128,32,16]{0,2,1:T(8,128)S(1)}, u32[]{:S(2)}, u32[]{:S(2)}) %all-to-all-start.1) | async-done | bytes 262176 | tf_op jit(solution)/shard_map/all_to_all | solution.py:134
  (1183 shorter events, 159.6 us)
Async XLA Ops:
  4.3 48.6 %all-to-all-start.2 = ((bf16[32,2,1024]{2,1,0:T(2,128)(2,1)}), bf16[32,2,1024]{2,1,0:T(2,128)(2,1)S(1)}, u32[]{:S(2)}, u32[]{:S(2)}) async-start(bf16[32,2,1024]{2,1,0:T(2,128)(2,1)} %reshape.1714), calls=%async_computation.2 | async-start | bytes 262144 | tf_op jit(solution)/shard_map/all_to_all | solution.py:100
  17.8 45.3 %copy-start.93 = (f32[512]{0:T(512)}, f32[512]{0:T(512)S(1)}, u32[]{:S(2)}) copy-start(f32[512]{0:T(512)S(1)} %neg.430) | copy-start | bytes 6148
  18.5 43.1 %copy-start.75 = (f32[512]{0:T(512)}, f32[512]{0:T(512)S(1)}, u32[]{:S(2)}) copy-start(f32[512]{0:T(512)S(1)} %get-tuple-element.261) | copy-start | bytes 6148
  18.5 48.4 %copy-start.92 = (f32[512]{0:T(512)}, f32[512]{0:T(512)S(1)}, u32[]{:S(2)}) copy-start(f32[512]{0:T(512)S(1)} %neg.427) | copy-start | bytes 6148
  18.6 64.0 %copy-start.83 = (f32[512]{0:T(512)}, f32[512]{0:T(512)S(1)}, u32[]{:S(2)}) copy-start(f32[512]{0:T(512)S(1)} %neg.424) | copy-start | bytes 6148
  18.7 52.2 %copy-start.85 = (f32[512]{0:T(512)}, f32[512]{0:T(512)S(1)}, u32[]{:S(2)}) copy-start(f32[512]{0:T(512)S(1)} %neg.415) | copy-start | bytes 6148
  18.8 67.7 %copy-start.87 = (f32[512]{0:T(512)}, f32[512]{0:T(512)S(1)}, u32[]{:S(2)}) copy-start(f32[512]{0:T(512)S(1)} %neg.412) | copy-start | bytes 6148
  18.9 55.9 %copy-start.88 = (f32[512]{0:T(512)}, f32[512]{0:T(512)S(1)}, u32[]{:S(2)}) copy-start(f32[512]{0:T(512)S(1)} %neg.418) | copy-start | bytes 6148
  19.0 59.7 %copy-start.90 = (f32[512]{0:T(512)}, f32[512]{0:T(512)S(1)}, u32[]{:S(2)}) copy-start(f32[512]{0:T(512)S(1)} %neg.421) | copy-start | bytes 6148
  19.1 42.5 %copy-start.94 = (f32[512]{0:T(512)}, f32[512]{0:T(512)S(1)}, u32[]{:S(2)}) copy-start(f32[512]{0:T(512)S(1)} %neg.409) | copy-start | bytes 6148
  19.7 41.9 %copy-start.77 = (f32[512]{0:T(512)}, f32[512]{0:T(512)S(1)}, u32[]{:S(2)}) copy-start(f32[512]{0:T(512)S(1)} %get-tuple-element.315) | copy-start | bytes 6148
  20.3 41.3 %copy-start.63 = (f32[512]{0:T(512)}, f32[512]{0:T(512)S(1)}, u32[]{:S(2)}) copy-start(f32[512]{0:T(512)S(1)} %get-tuple-element.324) | copy-start | bytes 6148
  20.3 41.3 %copy-start.65 = (f32[512]{0:T(512)}, f32[512]{0:T(512)S(1)}, u32[]{:S(2)}) copy-start(f32[512]{0:T(512)S(1)} %get-tuple-element.351) | copy-start | bytes 6148
  20.9 40.6 %copy-start.71 = (f32[512]{0:T(512)}, f32[512]{0:T(512)S(1)}, u32[]{:S(2)}) copy-start(f32[512]{0:T(512)S(1)} %get-tuple-element.279) | copy-start | bytes 6148
  20.9 40.7 %copy-start.73 = (f32[512]{0:T(512)}, f32[512]{0:T(512)S(1)}, u32[]{:S(2)}) copy-start(f32[512]{0:T(512)S(1)} %get-tuple-element.361) | copy-start | bytes 6148
  21.6 40.0 %copy-start.67 = (f32[512]{0:T(512)}, f32[512]{0:T(512)S(1)}, u32[]{:S(2)}) copy-start(f32[512]{0:T(512)S(1)} %get-tuple-element.288) | copy-start | bytes 6148
  21.6 40.0 %copy-start.69 = (f32[512]{0:T(512)}, f32[512]{0:T(512)S(1)}, u32[]{:S(2)}) copy-start(f32[512]{0:T(512)S(1)} %get-tuple-element.356) | copy-start | bytes 6148
  21.6 154.9 %copy-start.61 = (f32[512]{0:T(512)}, f32[512]{0:T(512)S(1)}, u32[]{:S(2)}) copy-start(f32[512]{0:T(512)S(1)} %get-tuple-element.289) | copy-start | bytes 6148
  52.9 39.7 %all-to-all-start = ((bf16[32,2,1024]{2,1,0:T(2,128)(2,1)}), bf16[32,2,1024]{2,1,0:T(2,128)(2,1)S(1)}, u32[]{:S(2)}, u32[]{:S(2)}) async-start(bf16[32,2,1024]{2,1,0:T(2,128)(2,1)} %reshape.1712), calls=%async_computation | async-start | bytes 262144 | tf_op jit(solution)/shard_map/all_to_all | solution.py:103
  236.6 53.0 %copy-start.39 = (f32[8,16]{1,0:T(8,128)S(1)}, f32[8,16]{1,0:T(8,128)}, u32[]{:S(2)}) copy-start(f32[8,16]{1,0:T(8,128)} %copy-done.38) | copy-start | bytes 1540
  236.6 54.7 %copy-start.62 = (f32[512]{0:T(512)S(1)}, f32[512]{0:T(512)}, u32[]{:S(2)}) copy-start(f32[512]{0:T(512)} %copy-done.61) | copy-start | bytes 6148
  238.4 55.8 %copy-start.33 = (f32[8,512]{1,0:T(8,128)S(1)}, f32[8,512]{1,0:T(8,128)}, u32[]{:S(2)}) copy-start(f32[8,512]{1,0:T(8,128)} %get-tuple-element.339) | copy-start | bytes 49156
  238.4 55.8 %copy-start.35 = (f32[8,512]{1,0:T(8,128)S(1)}, f32[8,512]{1,0:T(8,128)}, u32[]{:S(2)}) copy-start(f32[8,512]{1,0:T(8,128)} %get-tuple-element.341) | copy-start | bytes 49156
  300.8 26.1 %all-to-all-start.1 = ((f32[128,32,16]{0,2,1:T(8,128)}), f32[128,32,16]{0,2,1:T(8,128)S(1)}, u32[]{:S(2)}, u32[]{:S(2)}) async-start(f32[128,32,16]{0,2,1:T(8,128)} %copy.1032), calls=%async_computation.1 | async-start | bytes 524288 | tf_op jit(solution)/shard_map/all_to_all | solution.py:134
  (130 other events, 811.8 us)
where the time goes:
time: 335 us; the launch traced here: 328 us
  local copies, waits for them, and re-layouts  124 us (37%)
  matrix products  63.3 us (19%)
  blocking collectives  45.9 us (14%)
  other arithmetic  45.7 us (14%)
  starting transfers between devices  33.6 us (10%)
  waiting for transfers between devices  9.92 us (3%)
  between operations  5.76 us (2%)
    psum x1, blocking collectives, body(): totals = lax.psum(partial_value, 'dp')  45.9 us
    dot_general x8, matrix products, local_pass(): jnp.einsum('bic,ijc->bjc', block_grad, weights, precision=precise)  33.8 us
    dot_general x8, matrix products, local_pass(): fprev_in = jnp.einsum('bic,jic->bjc', block_in, weights, precision=precise)  29.5 us
    slice x176, local copies, waits for them, and re-layouts, local_pass(): lax.associative_scan(pair_combine, (block_decay, block_starts), reverse=T...  27.2 us
    dot_general x8, local copies, waits for them, and re-layouts, local_pass(): fprev_in = jnp.einsum('bic,jic->bjc', block_in, weights, precision=precise)  22 us
    all_to_all x1, starting transfers between devices, body(): lax.all_to_all(grads_rows.reshape(length, shards, narrow), 'ctx', split_a...  15 us
    dot_general x8, local copies, waits for them, and re-layouts, local_pass(): jnp.einsum('bic,ijc->bjc', block_grad, weights, precision=precise)  14 us
    all_to_all x1, starting transfers between devices, body(): lax.all_to_all(tokens[0].reshape(length, 1, channels), 'ctx', split_axis=...  10.2 us
  transfers between devices with their start and end apart: 3, of which 1 were waited for; matrix products, arithmetic and copies ran while one was open for 22% of the time, Pallas kernels for 0%

commit v1 on v0

v1 whole, which is shorter than its diff:
```python
import functools

import jax
import jax.numpy as jnp
from jax import lax
from jax.experimental import pallas as pl
from jax.experimental.pallas import tpu as pltpu
from jax.sharding import PartitionSpec as P

MESH = pl.DeviceIdType.MESH
MODES = 8
LANES = 128
GROUP = 16
RUNS = 8
RUN = 16
SIDE = 8


def roll(value, groups):
    return pltpu.roll(value, (groups * GROUP) % LANES, 1)


def lane_group():
    return lax.broadcasted_iota(jnp.int32, (8, LANES), 1) // GROUP


def swap_blocks(blocks):
    group = lane_group()
    blocks = list(blocks)
    for step in (4, 2, 1):
        low = (group // step) % 2 == 0
        for a in range(SIDE):
            if (a // step) % 2 == 0:
                first, second = blocks[a], blocks[a + step]
                blocks[a] = jnp.where(low, first, roll(second, step))
                blocks[a + step] = jnp.where(low, roll(first, -step), second)
    return blocks


def summarise(g, xs, cs, rates, factors, sums, lags, starts, tx):
    lanes = pl.ds(pl.multiple_of(g * LANES, LANES), LANES)
    x = [xs[g, pl.ds(i, RUNS, stride=RUN), :] for i in range(RUN)]
    c = [cs[g, pl.ds(i, RUNS, stride=RUN), :] for i in range(RUN)]
    for mode in range(MODES):
        factor = jnp.broadcast_to(factors[pl.ds(mode, 1), lanes], (RUNS, LANES))
        state, tail = x[0], jnp.zeros((RUNS, LANES), jnp.float32)
        for i in range(1, RUN):
            tail = factor * (tail + state)
            state = factor * state + x[i]
        adjoint, head = c[RUN - 1], jnp.zeros((RUNS, LANES), jnp.float32)
        for i in range(RUN - 2, -1, -1):
            head = factor * (head + adjoint)
            adjoint = factor * adjoint + c[i]
        rows = pl.ds(mode * RUNS, RUNS)
        sums[0, rows, :] = state
        sums[1, rows, :] = tail
        sums[2, rows, :] = adjoint
        sums[3, rows, :] = head + adjoint
    for lag in range(RUN):
        total = c[lag] * x[0]
        for i in range(1, RUN - lag):
            total = total + c[i + lag] * x[i]
        lags[pl.ds(lag, 1), :] = jnp.sum(total, axis=0, keepdims=True)
    rate = rates[:, lanes]
    factor = factors[:, lanes]
    power = jnp.exp(rate * -float(RUN))

    def spread(lag):
        return jnp.broadcast_to(lags[pl.ds(lag, 1), :], (MODES, LANES))

    zeros = jnp.zeros((MODES, LANES), jnp.float32)
    inner, cross = spread(RUN - 1), zeros
    for lag in range(RUN - 2, -1, -1):
        cross = factor * cross + inner
        inner = factor * inner + spread(lag)
    run = [[sums[q, pl.ds(a, MODES, stride=RUNS), :] for q in range(4)] for a in range(RUNS)]
    state, tail, outer = zeros, zeros, zeros
    befores = []
    for a in range(RUNS):
        run_state, run_tail, run_adjoint, run_head = run[a]
        befores.append(state)
        outer = outer + state * run_adjoint
        cross = cross + state * run_head
        tail = run_tail + power * (tail + float(RUN) * state)
        state = run_state + power * state
    adjoint, head = zeros, zeros
    for a in range(RUNS - 1, -1, -1):
        run_state, run_tail, run_adjoint, run_head = run[a]
        starts[g, pl.ds(a * MODES, MODES), :] = adjoint
        cross = cross + adjoint * (run_tail + (float(RUN) * power) * befores[a])
        head = run_head + power * (head + float(RUN) * adjoint)
        adjoint = run_adjoint + power * adjoint
    inner = inner + factor * outer
    tiles = swap_blocks([adjoint, state, head, state, inner, cross, spread(0), tail])
    for i in range(SIDE):
        tx[g * SIDE + i] = tiles[i]


def local_grads(g, cs, factors, residue, skip, starts, grads):
    lanes = pl.ds(pl.multiple_of(g * LANES, LANES), LANES)

    def row(ref, mode):
        return jnp.broadcast_to(ref[pl.ds(mode, 1), lanes], (RUNS, LANES))

    factor = [row(factors, mode) for mode in range(MODES)]
    weight = [row(residue, mode) for mode in range(MODES)]
    direct = row(skip, 0)
    adjoint = [starts[g, pl.ds(mode, RUNS, stride=MODES), :] for mode in range(MODES)]
    for i in range(RUN - 1, -1, -1):
        now = cs[g, pl.ds(i, RUNS, stride=RUN), :]
        total = direct * now
        for mode in range(MODES):
            adjoint[mode] = factor[mode] * adjoint[mode] + now
            total = total + weight[mode] * adjoint[mode]
        grads[g, pl.ds(i, RUNS, stride=RUN), :] = total


def own_lanes(value, place):
    value = jnp.where(lane_group() == place, value, 0.0)
    for step in (1, 2, 4):
        value = value + roll(value, step)
    return value


def owner_sums(place, block, length, positions, rates, residue, rx, zbuf):
    lanes = pl.ds(pl.multiple_of(block * LANES, LANES), LANES)
    rate = own_lanes(rates[:, lanes], place)
    weight = own_lanes(residue[:, lanes], place)
    factor = jnp.exp(-rate)
    power = jnp.exp(rate * -float(length))
    shards = rx.shape[0]
    zeros = jnp.zeros((MODES, LANES), jnp.float32)
    state, plain, by_state, by_adjoint, both = zeros, zeros, zeros, zeros, zeros
    befores = []
    for k in range(shards):
        tile = rx[k]
        befores.append(state)
        plain = plain + tile
        by_state = by_state + state * roll(tile, 1)
        state = power * state + tile
    adjoint = zeros
    for k in range(shards - 1, -1, -1):
        tile = rx[k]
        zbuf[pl.ds(k * MODES, MODES), :] = adjoint
        by_adjoint = by_adjoint + adjoint * roll(tile, 1)
        both = both + befores[k] * roll(adjoint, 1)
        adjoint = power * adjoint + tile
    scale = 1.0 / positions
    sum_residue = roll(plain, -4) + factor * roll(by_state, -1)
    sum_decay = roll(plain, -5) + roll(by_state, -3) + by_adjoint + (float(length) * power) * roll(both, -1)
    sum_skip = roll(plain, -6)
    last = [sum_residue * scale, (-scale) * factor * weight * sum_decay, sum_skip * scale]
    for k in range(SIDE):
        zbuf[pl.ds((shards + k) * MODES, MODES), :] = last[k] if k < len(last) else zeros


def pack_rows(zbuf, a):
    group = lane_group()
    packed = zbuf[pl.ds(a * SIDE * MODES, SIDE, stride=MODES), :]
    for mode in range(1, MODES):
        rows = zbuf[pl.ds(a * SIDE * MODES + mode, SIDE, stride=MODES), :]
        packed = jnp.where(group == mode, roll(rows, mode), packed)
    return packed


def unpack_rows(rows):
    apart = (lane_group() - lax.broadcasted_iota(jnp.int32, (8, LANES), 0) + SIDE) % SIDE
    out = rows
    for step in range(1, SIDE):
        moved = roll(pltpu.roll(rows, SIDE - step, 0), step)
        out = jnp.where(apart == step, moved, out)
    return out


def exchange_kernel(
    shards,
    groups,
    positions,
    tokens,
    cotangent,
    rates_in,
    residue_in,
    skip_in,
    grads,
    carry_out,
    totals_out,
    x_raw,
    c_raw,
    rates,
    residue,
    skip,
    xs,
    cs,
    factors,
    sums,
    lags,
    starts,
    tx,
    rx,
    zbuf,
    ztx,
    zrx,
    ptx,
    prx,
    in_sems,
    ctx_sems,
    back_sems,
    dp_sems,
):
    dp, ctx = lax.axis_index("dp"), lax.axis_index("ctx")
    length, channels = x_raw.shape
    blocks = channels // LANES
    loads = [
        pltpu.make_async_copy(source, target, in_sems.at[n])
        for n, (source, target) in enumerate(
            ((tokens, x_raw), (cotangent, c_raw), (rates_in, rates), (residue_in, residue), (skip_in, skip))
        )
    ]
    for load in loads:
        load.start()
    barrier = pltpu.get_barrier_semaphore()

    @pl.loop(1, shards)
    def _(d):
        pl.semaphore_signal(barrier, inc=1, device_id=(dp, lax.rem(ctx + d, shards)), device_id_type=MESH)

    @pl.loop(1, groups)
    def _(d):
        pl.semaphore_signal(barrier, inc=1, device_id=(lax.rem(dp + d, groups), ctx), device_id_type=MESH)

    for load in loads[2:]:
        load.wait()
    factors[...] = jnp.exp(-rates[...])
    for load, raw, wide in ((loads[0], x_raw, xs), (loads[1], c_raw, cs)):
        load.wait()
        for g in range(blocks):
            wide[g] = raw[:, pl.ds(g * LANES, LANES)].astype(jnp.float32)

    @pl.loop(0, blocks)
    def _(g):
        summarise(g, xs, cs, rates, factors, sums, lags, starts, tx)

    carry_out[pl.ds(MODES, MODES), :] = rates[...]
    rx[ctx] = tx[ctx]
    pl.semaphore_wait(barrier, shards + groups - 2)

    @pl.loop(1, shards)
    def _(d):
        peer = lax.rem(ctx + d, shards)
        pltpu.make_async_remote_copy(
            src_ref=tx.at[peer],
            dst_ref=rx.at[ctx],
            send_sem=ctx_sems.at[0],
            recv_sem=ctx_sems.at[1],
            device_id=(dp, peer),
            device_id_type=MESH,
        ).start()

    @pl.loop(0, blocks)
    def _(g):
        local_grads(g, cs, factors, residue, skip, starts, grads)

    most = pl.ds(0, shards - 1)
    pltpu.make_async_copy(rx.at[most], rx.at[most], ctx_sems.at[1]).wait()
    owner_sums(lax.rem(ctx, SIDE), ctx // SIDE, length, positions, rates, residue, rx, zbuf)
    ptx[...] = pack_rows(zbuf, shards // SIDE)
    prx[dp] = ptx[...]

    @pl.loop(1, groups)
    def _(d):
        pltpu.make_async_remote_copy(
            src_ref=ptx,
            dst_ref=prx.at[dp],
            send_sem=dp_sems.at[0],
            recv_sem=dp_sems.at[1],
            device_id=(lax.rem(dp + d, groups), ctx),
            device_id_type=MESH,
        ).start()

    for a in range(shards // SIDE):
        ztx[pl.ds(a * SIDE, SIDE)] = pack_rows(zbuf, a).reshape(SIDE, 1, LANES)
    zrx[ctx] = ztx[ctx]

    @pl.loop(1, shards)
    def _(d):
        peer = lax.rem(ctx + d, shards)
        pltpu.make_async_remote_copy(
            src_ref=ztx.at[peer],
            dst_ref=zrx.at[ctx],
            send_sem=back_sems.at[0],
            recv_sem=back_sems.at[1],
            device_id=(dp, peer),
            device_id_type=MESH,
        ).start()

    pltpu.make_async_copy(tx.at[most], tx.at[most], ctx_sems.at[0]).wait()
    pltpu.make_async_copy(zrx.at[most], zrx.at[most], back_sems.at[1]).wait()
    for g in range(blocks):
        rows = zrx[pl.ds(g * SIDE, SIDE)].reshape(SIDE, LANES)
        lanes = pl.ds(g * LANES, LANES)
        carry_out[pl.ds(0, MODES), lanes] = residue[:, lanes] * unpack_rows(rows)
    pltpu.make_async_copy(ztx.at[most], ztx.at[most], back_sems.at[0]).wait()
    others = pl.ds(0, groups - 1)
    pltpu.make_async_copy(prx.at[others], prx.at[others], dp_sems.at[1]).wait()
    total = prx[0]
    for n in range(1, groups):
        total = total + prx[n]
    totals_out[...] = total
    pltpu.make_async_copy(prx.at[others], prx.at[others], dp_sems.at[0]).wait()


def finish_kernel(grads, carry, totals, out, out_residue, out_decay, out_skip):
    blocks, length, _ = grads.shape
    ahead = (SIDE - lax.broadcasted_iota(jnp.int32, (8, LANES), 0)).astype(jnp.float32)
    for g in range(blocks):
        lanes = pl.ds(g * LANES, LANES)
        rate = [jnp.broadcast_to(carry[pl.ds(MODES + m, 1), lanes], (8, LANES)) for m in range(MODES)]
        power = [jnp.exp(rate[m] * -8.0) for m in range(MODES)]
        term = [
            jnp.exp(-rate[m] * ahead) * jnp.broadcast_to(carry[pl.ds(m, 1), lanes], (8, LANES))
            for m in range(MODES)
        ]
        for b in range(length // 8 - 1, -1, -1):
            rows = pl.ds(b * 8, 8)
            total = grads[g, rows, :]
            for m in range(MODES):
                total = total + term[m]
                if b:
                    term[m] = power[m] * term[m]
            out[rows, lanes] = total
    sublane = lax.broadcasted_iota(jnp.int32, (8, LANES), 0)
    for row, ref in ((0, out_residue), (1, out_decay)):
        spread = jnp.broadcast_to(totals[pl.ds(row, 1), :], (8, LANES))
        value = spread
        for m in range(1, MODES):
            value = jnp.where(sublane == m, roll(spread, -m), value)
        ref[...] = value[:, :GROUP]
    out_skip[...] = totals[2, :GROUP]


def body(shards, groups, tokens, cotangent, decay, residue, skip):
    _, length, channels = tokens.shape
    positions = float(length * shards * groups)
    blocks = channels // LANES
    vmem = pl.BlockSpec(memory_space=pltpu.VMEM)
    hbm = pl.BlockSpec(memory_space=pltpu.HBM)
    f32 = jnp.float32
    grads, carry, totals = pl.pallas_call(
        functools.partial(exchange_kernel, shards, groups, positions),
        out_shape=[
            jax.ShapeDtypeStruct((blocks, length, LANES), f32),
            jax.ShapeDtypeStruct((2 * MODES, channels), f32),
            jax.ShapeDtypeStruct((8, LANES), f32),
        ],
        in_specs=[hbm] * 5,
        out_specs=[vmem] * 3,
        scratch_shapes=[
            pltpu.VMEM((length, channels), jnp.bfloat16),
            pltpu.VMEM((length, channels), jnp.bfloat16),
            pltpu.VMEM((MODES, channels), f32),
            pltpu.VMEM((MODES, channels), f32),
            pltpu.VMEM((1, channels), f32),
            pltpu.VMEM((blocks, length, LANES), f32),
            pltpu.VMEM((blocks, length, LANES), f32),
            pltpu.VMEM((MODES, channels), f32),
            pltpu.VMEM((4, MODES * RUNS, LANES), f32),
            pltpu.VMEM((RUN, LANES), f32),
            pltpu.VMEM((blocks, RUNS * MODES, LANES), f32),
            pltpu.VMEM((shards, 8, LANES), f32),
            pltpu.VMEM((shards, 8, LANES), f32),
            pltpu.VMEM(((shards + SIDE) * MODES, LANES), f32),
            pltpu.VMEM((shards, 1, LANES), f32),
            pltpu.VMEM((shards, 1, LANES), f32),
            pltpu.VMEM((8, LANES), f32),
            pltpu.VMEM((groups, 8, LANES), f32),
            pltpu.SemaphoreType.DMA((5,)),
            pltpu.SemaphoreType.DMA((2,)),
            pltpu.SemaphoreType.DMA((2,)),
            pltpu.SemaphoreType.DMA((2,)),
        ],
        compiler_params=pltpu.CompilerParams(
            collective_id=1, has_side_effects=True, vmem_limit_bytes=32 * 1024 * 1024
        ),
        name="exchange",
    )(tokens[0], cotangent[0], decay, residue, skip.reshape(1, channels))
    out, grad_residue, grad_decay, grad_skip = pl.pallas_call(
        finish_kernel,
        out_shape=[
            jax.ShapeDtypeStruct((length, channels), f32),
            jax.ShapeDtypeStruct((MODES, GROUP), f32),
            jax.ShapeDtypeStruct((MODES, GROUP), f32),
            jax.ShapeDtypeStruct((GROUP,), f32),
        ],
        in_specs=[vmem] * 3,
        out_specs=[vmem] * 4,
        compiler_params=pltpu.CompilerParams(vmem_limit_bytes=32 * 1024 * 1024),
        name="finish",
    )(grads, carry, totals)
    return out[None], grad_residue, grad_decay, grad_skip


def solution(mesh):
    return jax.shard_map(
        functools.partial(body, mesh.shape["ctx"], mesh.shape["dp"]),
        mesh=mesh,
        in_specs=(P("dp", "ctx", None), P("dp", "ctx", None), P(), P(), P()),
        out_specs=(P("dp", "ctx", None), P(None, "ctx"), P(None, "ctx"), P("ctx")),
        check_vma=False,
    )
```

time: 335 us -> 29.4 us (0.09); the launches traced: 328 us -> 29.1 us
  local copies, waits for them, and re-layouts: 124 us -> 3.92 us
  matrix products: 63.3 us -> 0 us
  blocking collectives: 45.9 us -> 0 us
  other arithmetic: 45.7 us -> 0 us
  starting transfers between devices: 33.6 us -> 0 us
  Pallas kernels: 0 us -> 24.5 us
  waiting for transfers between devices: 9.92 us -> 0 us
  between operations: 5.76 us -> 0.65 us
    dot_general x16 -> x0, matrix products: 63.3 us -> none  [the longest x8 33.8 us: local_pass(): jnp.einsum('bic,ijc->bjc', block_grad, weights, precision=precise)]
    psum x1 -> x0, blocking collectives: 45.9 us -> none  [body(): totals = lax.psum(partial_value, 'dp')]
    slice x309 -> x0, local copies, waits for them, and re-layouts: 36.2 us -> none  [the longest x176 27.2 us: local_pass(): lax.associative_scan(pair_combine, (block_decay, block_starts), reverse=T...]
    dot_general x16 -> x0, local copies, waits for them, and re-layouts: 36 us -> none  [the longest x8 22 us: local_pass(): fprev_in = jnp.einsum('bic,jic->bjc', block_in, weights, precision=precise)]
    all_to_all x3 -> x0, starting transfers between devices: 33.6 us -> none  [the longest x1 15 us: body(): lax.all_to_all(grads_rows.reshape(length, shards, narrow), 'ctx', split_a...]
    pallas_call x0 -> x2, Pallas kernels: none -> 24.5 us  [the longest x1 23.7 us: body(): pl.pallas_call(functools.partial(exchange_kernel, shards, groups, positio...]
    mul x25 -> x0, local copies, waits for them, and re-layouts: 21.1 us -> none  [the longest x8 8.28 us: finish(): jnp.exp(-rate * block_len * (nblocks - 1 - block_index)) * end_state[mode]]
    add x159 -> x0, other arithmetic: 13.4 us -> none  [the longest x2 3.02 us: local_pass(): block_ends = factor * fprev_in[:, -1] + block_in[:, -1]]
  transfers between devices with their start and end apart: 3 -> 0, of which waited for: 1 -> 0; matrix products, arithmetic and copies ran while one was open for 22% -> 0% of each run, Pallas kernels for 0% -> 0%
where the time goes in v1:
time: 29.4 us; the launch traced here: 29.1 us
  Pallas kernels  24.5 us (83%)
  local copies, waits for them, and re-layouts  3.92 us (13%)
  between operations  0.65 us (2%)
    pallas_call x1, Pallas kernels, body(): pl.pallas_call(functools.partial(exchange_kernel, shards, groups, positio...  23.7 us
    unnamed x10, local copies, waits for them, and re-layouts  3.92 us
    pallas_call x1, Pallas kernels, body(): pl.pallas_call(finish_kernel, out_shape=[jax.ShapeDtypeStruct((length, ch...  0.89 us

profile of v1, /device:TPU:1, one launch (start us, length us, event | category | flops | bytes accessed | tf_op | source)
XLA Modules:
  0.0 29.1 jit_solution(4067529994911010916)
XLA Ops:
  0.6 0.0 copy-start.4
  0.6 0.7 %copy-done.4 = f32[512]{0:T(512)S(1)} copy-done((f32[512]{0:T(512)S(1)}, f32[512]{0:T(512)}, u32[]{:S(2)}) %copy-start.4) | copy-done | bytes 2072
  1.3 0.0 copy-start
  1.3 0.9 %copy-done = bf16[1,128,512]{2,1,0:T(8,128)(2,1)S(1)} copy-done((bf16[1,128,512]{2,1,0:T(8,128)(2,1)S(1)}, bf16[1,128,512]{2,1,0:T(8,128)(2,1)}, u32[]{:S(2)}) %copy-start) | copy-done | bytes 131096
  2.2 0.0 copy-start.1
  2.2 0.9 %copy-done.1 = bf16[1,128,512]{2,1,0:T(8,128)(2,1)S(1)} copy-done((bf16[1,128,512]{2,1,0:T(8,128)(2,1)S(1)}, bf16[1,128,512]{2,1,0:T(8,128)(2,1)}, u32[]{:S(2)}) %copy-start.1) | copy-done | bytes 131096
  3.1 0.0 copy-start.2
  3.1 0.7 %copy-done.2 = f32[8,512]{1,0:T(8,128)S(1)} copy-done((f32[8,512]{1,0:T(8,128)S(1)}, f32[8,512]{1,0:T(8,128)}, u32[]{:S(2)}) %copy-start.2) | copy-done | bytes 16408
  3.8 0.0 copy-start.3
  3.8 0.7 %copy-done.3 = f32[8,512]{1,0:T(8,128)S(1)} copy-done((f32[8,512]{1,0:T(8,128)S(1)}, f32[8,512]{1,0:T(8,128)}, u32[]{:S(2)}) %copy-start.3) | copy-done | bytes 16408
  4.6 23.7 %exchange.1 = (f32[4,128,128]{2,1,0:T(8,128)S(1)}, f32[16,512]{1,0:T(8,128)S(1)}, f32[8,128]{1,0:T(8,128)S(1)}) custom-call(bf16[128,512]{1,0:T(8,128)(2,1)S(1)} %bitcast.4, bf16[128,512]{1,0:T(8,128)(2,1)S(1)} %bitcast.5, f32[8,512]{1,0:T(8,128)S(1)} %copy-done.2, f32[8,512]{1,0:T(8,128)S(1)} %copy-done.3, f32[1,512]{1,0:T(1,128)S(1)} %bitcast.6), custom_call_target="tpu_custom_call" | custom-call | tf_op jit(solution)/shard_map/exchange/pallas_call | solution.py:348
  28.2 0.9 %finish.1 = (f32[128,512]{1,0:T(8,128)}, f32[8,16]{1,0:T(8,128)}, f32[8,16]{1,0:T(8,128)}, f32[16]{0:T(128)}) custom-call(f32[4,128,128]{2,1,0:T(8,128)S(1)} %get-tuple-element.11.grads, f32[16,512]{1,0:T(8,128)S(1)} %get-tuple-element.12.carry, f32[8,128]{1,0:T(8,128)S(1)} %get-tuple-element.13.totals), custom_call_target="tpu_custom_call" | custom-call | tf_op jit(solution)/shard_map/finish/pallas_call | solution.py:386
Async XLA Ops:
  0.6 0.7 %copy-start.4 = (f32[512]{0:T(512)S(1)}, f32[512]{0:T(512)}, u32[]{:S(2)}) copy-start(f32[512]{0:T(512)} %param.9) | copy-start | bytes 6148
  1.3 0.9 %copy-start = (bf16[1,128,512]{2,1,0:T(8,128)(2,1)S(1)}, bf16[1,128,512]{2,1,0:T(8,128)(2,1)}, u32[]{:S(2)}) copy-start(bf16[1,128,512]{2,1,0:T(8,128)(2,1)} %param.5) | copy-start | bytes 393220
  2.2 0.9 %copy-start.1 = (bf16[1,128,512]{2,1,0:T(8,128)(2,1)S(1)}, bf16[1,128,512]{2,1,0:T(8,128)(2,1)}, u32[]{:S(2)}) copy-start(bf16[1,128,512]{2,1,0:T(8,128)(2,1)} %param.6) | copy-start | bytes 393220
  3.1 0.7 %copy-start.2 = (f32[8,512]{1,0:T(8,128)S(1)}, f32[8,512]{1,0:T(8,128)}, u32[]{:S(2)}) copy-start(f32[8,512]{1,0:T(8,128)} %rates_in.1) | copy-start | bytes 49156
  3.8 0.7 %copy-start.3 = (f32[8,512]{1,0:T(8,128)S(1)}, f32[8,512]{1,0:T(8,128)}, u32[]{:S(2)}) copy-start(f32[8,512]{1,0:T(8,128)} %residue_in.1) | copy-start | bytes 49156

commit v2 on v1

--- a/solution.py
+++ b/solution.py
@@ -181,7 +181,7 @@
     rates_in,
     residue_in,
     skip_in,
-    grads,
+    grads_out,
     carry_out,
     totals_out,
     x_raw,
@@ -202,7 +202,11 @@
     zrx,
     ptx,
     prx,
+    grads,
+    carry,
+    totals,
     in_sems,
+    out_sems,
     ctx_sems,
     back_sems,
     dp_sems,
@@ -216,8 +220,6 @@
             ((tokens, x_raw), (cotangent, c_raw), (rates_in, rates), (residue_in, residue), (skip_in, skip))
         )
     ]
-    for load in loads:
-        load.start()
     barrier = pltpu.get_barrier_semaphore()
 
     @pl.loop(1, shards)
@@ -228,6 +230,8 @@
     def _(d):
         pl.semaphore_signal(barrier, inc=1, device_id=(lax.rem(dp + d, groups), ctx), device_id_type=MESH)
 
+    for load in loads:
+        load.start()
     for load in loads[2:]:
         load.wait()
     factors[...] = jnp.exp(-rates[...])
@@ -240,7 +244,7 @@
     def _(g):
         summarise(g, xs, cs, rates, factors, sums, lags, starts, tx)
 
-    carry_out[pl.ds(MODES, MODES), :] = rates[...]
+    carry[pl.ds(MODES, MODES), :] = rates[...]
     rx[ctx] = tx[ctx]
     pl.semaphore_wait(barrier, shards + groups - 2)
 
@@ -260,6 +264,11 @@
     def _(g):
         local_grads(g, cs, factors, residue, skip, starts, grads)
 
+    stores = [
+        pltpu.make_async_copy(source, target, out_sems.at[n])
+        for n, (source, target) in enumerate(((grads, grads_out), (carry, carry_out), (totals, totals_out)))
+    ]
+    stores[0].start()
     most = pl.ds(0, shards - 1)
     pltpu.make_async_copy(rx.at[most], rx.at[most], ctx_sems.at[1]).wait()
     owner_sums(lax.rem(ctx, SIDE), ctx // SIDE, length, positions, rates, residue, rx, zbuf)
@@ -298,15 +307,19 @@
     for g in range(blocks):
         rows = zrx[pl.ds(g * SIDE, SIDE)].reshape(SIDE, LANES)
         lanes = pl.ds(g * LANES, LANES)
-        carry_out[pl.ds(0, MODES), lanes] = residue[:, lanes] * unpack_rows(rows)
+        carry[pl.ds(0, MODES), lanes] = residue[:, lanes] * unpack_rows(rows)
+    stores[1].start()
     pltpu.make_async_copy(ztx.at[most], ztx.at[most], back_sems.at[0]).wait()
     others = pl.ds(0, groups - 1)
     pltpu.make_async_copy(prx.at[others], prx.at[others], dp_sems.at[1]).wait()
     total = prx[0]
     for n in range(1, groups):
         total = total + prx[n]
-    totals_out[...] = total
+    totals[...] = total
+    stores[2].start()
     pltpu.make_async_copy(prx.at[others], prx.at[others], dp_sems.at[0]).wait()
+    for store in stores:
+        store.wait()
 
 
 def finish_kernel(grads, carry, totals, out, out_residue, out_decay, out_skip):
@@ -353,7 +366,7 @@
             jax.ShapeDtypeStruct((8, LANES), f32),
         ],
         in_specs=[hbm] * 5,
-        out_specs=[vmem] * 3,
+        out_specs=[hbm] * 3,
         scratch_shapes=[
             pltpu.VMEM((length, channels), jnp.bfloat16),
             pltpu.VMEM((length, channels), jnp.bfloat16),
@@ -373,13 +386,17 @@
             pltpu.VMEM((shards, 1, LANES), f32),
             pltpu.VMEM((8, LANES), f32),
             pltpu.VMEM((groups, 8, LANES), f32),
+            pltpu.VMEM((blocks, length, LANES), f32),
+            pltpu.VMEM((2 * MODES, channels), f32),
+            pltpu.VMEM((8, LANES), f32),
             pltpu.SemaphoreType.DMA((5,)),
+            pltpu.SemaphoreType.DMA((3,)),
             pltpu.SemaphoreType.DMA((2,)),
             pltpu.SemaphoreType.DMA((2,)),
             pltpu.SemaphoreType.DMA((2,)),
         ],
         compiler_params=pltpu.CompilerParams(
-            collective_id=1, has_side_effects=True, vmem_limit_bytes=32 * 1024 * 1024
+            collective_id=1, has_side_effects=True, vmem_limit_bytes=60 * 1024 * 1024
         ),
         name="exchange",
     )(tokens[0], cotangent[0], decay, residue, skip.reshape(1, channels))
@@ -393,7 +410,7 @@
         ],
         in_specs=[vmem] * 3,
         out_specs=[vmem] * 4,
-        compiler_params=pltpu.CompilerParams(vmem_limit_bytes=32 * 1024 * 1024),
+        compiler_params=pltpu.CompilerParams(vmem_limit_bytes=60 * 1024 * 1024),
         name="finish",
     )(grads, carry, totals)
     return out[None], grad_residue, grad_decay, grad_skip

time: 29.4 us -> 26.7 us (0.908)
  local copies, waits for them, and re-layouts: 3.92 us -> 0 us
  Pallas kernels: 24.5 us -> 25.9 us
    unnamed x10 -> x0, local copies, waits for them, and re-layouts: 3.92 us -> none
    pallas_call x1, Pallas kernels: 0.89 us -> 1.86 us  [body(): pl.pallas_call(finish_kernel, out_shape=[jax.ShapeDtypeStruct((length, ch...]
    pallas_call x1, Pallas kernels: 23.7 us -> 24.1 us  [body(): pl.pallas_call(functools.partial(exchange_kernel, shards, groups, positio...]
where the time goes in v2:
time: 26.7 us; the launch traced here: 26.6 us
  Pallas kernels  25.9 us (97%)
  between operations  0.64 us (2%)
    pallas_call x1, Pallas kernels, body(): pl.pallas_call(functools.partial(exchange_kernel, shards, groups, positio...  24.1 us
    pallas_call x1, Pallas kernels, body(): pl.pallas_call(finish_kernel, out_shape=[jax.ShapeDtypeStruct((length, ch...  1.86 us

profile of v2, /device:TPU:1, one launch (start us, length us, event | category | flops | bytes accessed | tf_op | source)
XLA Modules:
  0.0 26.6 jit_solution(1703409922346706324)
XLA Ops:
  0.6 24.1 %exchange.1 = (f32[4,128,128]{2,1,0:T(8,128)}, f32[16,512]{1,0:T(8,128)}, f32[8,128]{1,0:T(8,128)}) custom-call(bf16[128,512]{1,0:T(8,128)(2,1)} %bitcast.4, bf16[128,512]{1,0:T(8,128)(2,1)} %bitcast.5, f32[8,512]{1,0:T(8,128)} %rates_in.1, f32[8,512]{1,0:T(8,128)} %residue_in.1, f32[1,512]{1,0:T(1,128)} %bitcast.6), custom_call_target="tpu_custom_call" | custom-call | tf_op jit(solution)/shard_map/exchange/pallas_call | solution.py:361
  24.7 1.9 %finish.1 = (f32[128,512]{1,0:T(8,128)}, f32[8,16]{1,0:T(8,128)}, f32[8,16]{1,0:T(8,128)}, f32[16]{0:T(128)}) custom-call(f32[4,128,128]{2,1,0:T(8,128)} %get-tuple-element.11.grads, f32[16,512]{1,0:T(8,128)} %get-tuple-element.12.carry, f32[8,128]{1,0:T(8,128)} %get-tuple-element.13.totals), custom_call_target="tpu_custom_call" | custom-call | tf_op jit(solution)/shard_map/finish/pallas_call | solution.py:403

commit v3 on v2

--- a/solution.py
+++ b/solution.py
@@ -14,6 +14,7 @@
 RUNS = 8
 RUN = 16
 SIDE = 8
+PLANE = 8
 
 
 def roll(value, groups):
@@ -210,6 +211,7 @@
     ctx_sems,
     back_sems,
     dp_sems,
+    ready_sem,
 ):
     dp, ctx = lax.axis_index("dp"), lax.axis_index("ctx")
     length, channels = x_raw.shape
@@ -220,15 +222,37 @@
             ((tokens, x_raw), (cotangent, c_raw), (rates_in, rates), (residue_in, residue), (skip_in, skip))
         )
     ]
+    half = groups // 2
+    late = dp // half
+    place_x = lax.rem(dp, half)
+    mirror = (shards // PLANE - 1 - ctx // PLANE) * PLANE + lax.rem(ctx, PLANE)
+    owned = ctx + late * (mirror - ctx)
+
+    def same_half(d):
+        return late * half + lax.rem(place_x + d, half)
+
+    def other_half(d):
+        return (1 - late) * half + d
+
     barrier = pltpu.get_barrier_semaphore()
+
+    def greet(group, peer):
+        pl.semaphore_signal(barrier, inc=1, device_id=(group, peer), device_id_type=MESH)
 
     @pl.loop(1, shards)
     def _(d):
-        pl.semaphore_signal(barrier, inc=1, device_id=(dp, lax.rem(ctx + d, shards)), device_id_type=MESH)
-
-    @pl.loop(1, groups)
+        greet(dp, lax.rem(ctx + d, shards))
+
+    @pl.loop(1, half)
     def _(d):
-        pl.semaphore_signal(barrier, inc=1, device_id=(lax.rem(dp + d, groups), ctx), device_id_type=MESH)
+        greet(same_half(d), owned)
+
+    @pl.when(late == 0)
+    def _():
+        @pl.loop(0, half)
+        def _(d):
+            greet(other_half(d), mirror)
+            greet(other_half(d), ctx)
 
     for load in loads:
         load.start()
@@ -245,14 +269,21 @@
         summarise(g, xs, cs, rates, factors, sums, lags, starts, tx)
 
     carry[pl.ds(MODES, MODES), :] = rates[...]
-    rx[ctx] = tx[ctx]
-    pl.semaphore_wait(barrier, shards + groups - 2)
+    rx[ctx] = tx[owned]
+    pl.semaphore_wait(barrier, shards - 1 + half - 1 + late * 2 * half)
+
+    @pl.when(late == 1)
+    def _():
+        @pl.loop(0, half)
+        def _(d):
+            pl.semaphore_signal(ready_sem, inc=1, device_id=(other_half(d), ctx), device_id_type=MESH)
 
     @pl.loop(1, shards)
     def _(d):
         peer = lax.rem(ctx + d, shards)
+        across = (shards // PLANE - 1 - peer // PLANE) * PLANE + lax.rem(peer, PLANE)
         pltpu.make_async_remote_copy(
-            src_ref=tx.at[peer],
+            src_ref=tx.at[peer + late * (across - peer)],
             dst_ref=rx.at[ctx],
             send_sem=ctx_sems.at[0],
             recv_sem=ctx_sems.at[1],
@@ -271,31 +302,50 @@
     stores[0].start()
     most = pl.ds(0, shards - 1)
     pltpu.make_async_copy(rx.at[most], rx.at[most], ctx_sems.at[1]).wait()
-    owner_sums(lax.rem(ctx, SIDE), ctx // SIDE, length, positions, rates, residue, rx, zbuf)
+    owner_sums(lax.rem(owned, SIDE), owned // SIDE, length, positions, rates, residue, rx, zbuf)
     ptx[...] = pack_rows(zbuf, shards // SIDE)
-    prx[dp] = ptx[...]
-
-    @pl.loop(1, groups)
-    def _(d):
+
+    def send_totals(group):
         pltpu.make_async_remote_copy(
             src_ref=ptx,
             dst_ref=prx.at[dp],
             send_sem=dp_sems.at[0],
             recv_sem=dp_sems.at[1],
-            device_id=(lax.rem(dp + d, groups), ctx),
+            device_id=(group, owned),
             device_id_type=MESH,
         ).start()
 
+    @pl.when(late == 1)
+    def _():
+        @pl.loop(0, half)
+        def _(d):
+            send_totals(other_half(d))
+
+        send_totals(dp)
+
+    @pl.loop(1, half)
+    def _(d):
+        send_totals(same_half(d))
+
+    @pl.when(late == 0)
+    def _():
+        prx[dp] = ptx[...]
+        pl.semaphore_wait(ready_sem, half)
+
+        @pl.loop(0, half)
+        def _(d):
+            send_totals(other_half(d))
+
     for a in range(shards // SIDE):
         ztx[pl.ds(a * SIDE, SIDE)] = pack_rows(zbuf, a).reshape(SIDE, 1, LANES)
-    zrx[ctx] = ztx[ctx]
+    zrx[owned] = ztx[ctx]
 
     @pl.loop(1, shards)
     def _(d):
         peer = lax.rem(ctx + d, shards)
         pltpu.make_async_remote_copy(
             src_ref=ztx.at[peer],
-            dst_ref=zrx.at[ctx],
+            dst_ref=zrx.at[owned],
             send_sem=back_sems.at[0],
             recv_sem=back_sems.at[1],
             device_id=(dp, peer),
@@ -310,14 +360,24 @@
         carry[pl.ds(0, MODES), lanes] = residue[:, lanes] * unpack_rows(rows)
     stores[1].start()
     pltpu.make_async_copy(ztx.at[most], ztx.at[most], back_sems.at[0]).wait()
-    others = pl.ds(0, groups - 1)
-    pltpu.make_async_copy(prx.at[others], prx.at[others], dp_sems.at[1]).wait()
+
+    def wait_totals(sem):
+        @pl.when(late == 1)
+        def _():
+            pltpu.make_async_copy(prx, prx, sem).wait()
+
+        @pl.when(late == 0)
+        def _():
+            others = pl.ds(0, groups - 1)
+            pltpu.make_async_copy(prx.at[others], prx.at[others], sem).wait()
+
+    wait_totals(dp_sems.at[1])
     total = prx[0]
     for n in range(1, groups):
         total = total + prx[n]
     totals[...] = total
     stores[2].start()
-    pltpu.make_async_copy(prx.at[others], prx.at[others], dp_sems.at[0]).wait()
+    wait_totals(dp_sems.at[0])
     for store in stores:
         store.wait()
 
@@ -394,6 +454,7 @@
             pltpu.SemaphoreType.DMA((2,)),
             pltpu.SemaphoreType.DMA((2,)),
             pltpu.SemaphoreType.DMA((2,)),
+            pltpu.SemaphoreType.REGULAR,
         ],
         compiler_params=pltpu.CompilerParams(
             collective_id=1, has_side_effects=True, vmem_limit_bytes=60 * 1024 * 1024

time: 26.7 us -> 25.2 us (0.944)
  Pallas kernels: 25.9 us -> 24.5 us
    pallas_call x1, Pallas kernels: 24.1 us -> 22.6 us  [body(): pl.pallas_call(functools.partial(exchange_kernel, shards, groups, positio...]
where the time goes in v3:
time: 25.2 us; the launch traced here: 25.1 us
  Pallas kernels  24.5 us (97%)
  between operations  0.64 us (3%)
    pallas_call x1, Pallas kernels, body(): pl.pallas_call(functools.partial(exchange_kernel, shards, groups, positio...  22.6 us
    pallas_call x1, Pallas kernels, body(): pl.pallas_call(finish_kernel, out_shape=[jax.ShapeDtypeStruct((length, ch...  1.86 us

profile of v3, /device:TPU:1, one launch (start us, length us, event | category | flops | bytes accessed | tf_op | source)
XLA Modules:
  0.0 25.1 jit_solution(2900896752345201189)
XLA Ops:
  0.6 22.6 %exchange.1 = (f32[4,128,128]{2,1,0:T(8,128)}, f32[16,512]{1,0:T(8,128)}, f32[8,128]{1,0:T(8,128)}) custom-call(bf16[128,512]{1,0:T(8,128)(2,1)} %bitcast.4, bf16[128,512]{1,0:T(8,128)(2,1)} %bitcast.5, f32[8,512]{1,0:T(8,128)} %rates_in.1, f32[8,512]{1,0:T(8,128)} %residue_in.1, f32[1,512]{1,0:T(1,128)} %bitcast.6), custom_call_target="tpu_custom_call" | custom-call | tf_op jit(solution)/shard_map/exchange/pallas_call | solution.py:421
  23.2 1.9 %finish.1 = (f32[128,512]{1,0:T(8,128)}, f32[8,16]{1,0:T(8,128)}, f32[8,16]{1,0:T(8,128)}, f32[16]{0:T(128)}) custom-call(f32[4,128,128]{2,1,0:T(8,128)} %get-tuple-element.11.grads, f32[16,512]{1,0:T(8,128)} %get-tuple-element.12.carry, f32[8,128]{1,0:T(8,128)} %get-tuple-element.13.totals), custom_call_target="tpu_custom_call" | custom-call | tf_op jit(solution)/shard_map/finish/pallas_call | solution.py:464

commit v4 on v3

--- a/solution.py
+++ b/solution.py
@@ -183,8 +183,8 @@
     residue_in,
     skip_in,
     grads_out,
-    carry_out,
-    totals_out,
+    zrx,
+    prx,
     x_raw,
     c_raw,
     rates,
@@ -200,12 +200,8 @@
     rx,
     zbuf,
     ztx,
-    zrx,
     ptx,
-    prx,
     grads,
-    carry,
-    totals,
     in_sems,
     out_sems,
     ctx_sems,
@@ -222,6 +218,8 @@
             ((tokens, x_raw), (cotangent, c_raw), (rates_in, rates), (residue_in, residue), (skip_in, skip))
         )
     ]
+    for load in loads:
+        load.start()
     half = groups // 2
     late = dp // half
     place_x = lax.rem(dp, half)
@@ -254,8 +252,6 @@
             greet(other_half(d), mirror)
             greet(other_half(d), ctx)
 
-    for load in loads:
-        load.start()
     for load in loads[2:]:
         load.wait()
     factors[...] = jnp.exp(-rates[...])
@@ -268,7 +264,6 @@
     def _(g):
         summarise(g, xs, cs, rates, factors, sums, lags, starts, tx)
 
-    carry[pl.ds(MODES, MODES), :] = rates[...]
     rx[ctx] = tx[owned]
     pl.semaphore_wait(barrier, shards - 1 + half - 1 + late * 2 * half)
 
@@ -295,11 +290,8 @@
     def _(g):
         local_grads(g, cs, factors, residue, skip, starts, grads)
 
-    stores = [
-        pltpu.make_async_copy(source, target, out_sems.at[n])
-        for n, (source, target) in enumerate(((grads, grads_out), (carry, carry_out), (totals, totals_out)))
-    ]
-    stores[0].start()
+    store = pltpu.make_async_copy(grads, grads_out, out_sems.at[0])
+    store.start()
     most = pl.ds(0, shards - 1)
     pltpu.make_async_copy(rx.at[most], rx.at[most], ctx_sems.at[1]).wait()
     owner_sums(lax.rem(owned, SIDE), owned // SIDE, length, positions, rates, residue, rx, zbuf)
@@ -327,18 +319,8 @@
     def _(d):
         send_totals(same_half(d))
 
-    @pl.when(late == 0)
-    def _():
-        prx[dp] = ptx[...]
-        pl.semaphore_wait(ready_sem, half)
-
-        @pl.loop(0, half)
-        def _(d):
-            send_totals(other_half(d))
-
     for a in range(shards // SIDE):
         ztx[pl.ds(a * SIDE, SIDE)] = pack_rows(zbuf, a).reshape(SIDE, 1, LANES)
-    zrx[owned] = ztx[ctx]
 
     @pl.loop(1, shards)
     def _(d):
@@ -352,13 +334,23 @@
             device_id_type=MESH,
         ).start()
 
+    @pl.when(late == 0)
+    def _():
+        keep = pltpu.make_async_copy(ptx, prx.at[dp], out_sems.at[1])
+        keep.start()
+        keep.wait()
+        pl.semaphore_wait(ready_sem, half)
+
+        @pl.loop(0, half)
+        def _(d):
+            send_totals(other_half(d))
+
+    keep_row = pltpu.make_async_copy(ztx.at[ctx], zrx.at[owned], out_sems.at[2])
+    keep_row.start()
     pltpu.make_async_copy(tx.at[most], tx.at[most], ctx_sems.at[0]).wait()
+    store.wait()
+    keep_row.wait()
     pltpu.make_async_copy(zrx.at[most], zrx.at[most], back_sems.at[1]).wait()
-    for g in range(blocks):
-        rows = zrx[pl.ds(g * SIDE, SIDE)].reshape(SIDE, LANES)
-        lanes = pl.ds(g * LANES, LANES)
-        carry[pl.ds(0, MODES), lanes] = residue[:, lanes] * unpack_rows(rows)
-    stores[1].start()
     pltpu.make_async_copy(ztx.at[most], ztx.at[most], back_sems.at[0]).wait()
 
     def wait_totals(sem):
@@ -372,25 +364,19 @@
             pltpu.make_async_copy(prx.at[others], prx.at[others], sem).wait()
 
     wait_totals(dp_sems.at[1])
-    total = prx[0]
-    for n in range(1, groups):
-        total = total + prx[n]
-    totals[...] = total
-    stores[2].start()
     wait_totals(dp_sems.at[0])
-    for store in stores:
-        store.wait()
-
-
-def finish_kernel(grads, carry, totals, out, out_residue, out_decay, out_skip):
+
+
+def finish_kernel(grads, zrx, prx, rates, residue, out, out_residue, out_decay, out_skip):
     blocks, length, _ = grads.shape
     ahead = (SIDE - lax.broadcasted_iota(jnp.int32, (8, LANES), 0)).astype(jnp.float32)
     for g in range(blocks):
         lanes = pl.ds(g * LANES, LANES)
-        rate = [jnp.broadcast_to(carry[pl.ds(MODES + m, 1), lanes], (8, LANES)) for m in range(MODES)]
+        rate = [jnp.broadcast_to(rates[pl.ds(m, 1), lanes], (8, LANES)) for m in range(MODES)]
         power = [jnp.exp(rate[m] * -8.0) for m in range(MODES)]
+        start = residue[:, lanes] * unpack_rows(zrx[pl.ds(g * SIDE, SIDE)].reshape(SIDE, LANES))
         term = [
-            jnp.exp(-rate[m] * ahead) * jnp.broadcast_to(carry[pl.ds(m, 1), lanes], (8, LANES))
+            jnp.exp(-rate[m] * ahead) * jnp.broadcast_to(start[m : m + 1], (8, LANES))
             for m in range(MODES)
         ]
         for b in range(length // 8 - 1, -1, -1):
@@ -401,9 +387,12 @@
                 if b:
                     term[m] = power[m] * term[m]
             out[rows, lanes] = total
+    totals = prx[0]
+    for n in range(1, prx.shape[0]):
+        totals = totals + prx[n]
     sublane = lax.broadcasted_iota(jnp.int32, (8, LANES), 0)
     for row, ref in ((0, out_residue), (1, out_decay)):
-        spread = jnp.broadcast_to(totals[pl.ds(row, 1), :], (8, LANES))
+        spread = jnp.broadcast_to(totals[row : row + 1], (8, LANES))
         value = spread
         for m in range(1, MODES):
             value = jnp.where(sublane == m, roll(spread, -m), value)
@@ -422,8 +411,8 @@
         functools.partial(exchange_kernel, shards, groups, positions),
         out_shape=[
             jax.ShapeDtypeStruct((blocks, length, LANES), f32),
-            jax.ShapeDtypeStruct((2 * MODES, channels), f32),
-            jax.ShapeDtypeStruct((8, LANES), f32),
+            jax.ShapeDtypeStruct((shards, 1, LANES), f32),
+            jax.ShapeDtypeStruct((groups, 8, LANES), f32),
         ],
         in_specs=[hbm] * 5,
         out_specs=[hbm] * 3,
@@ -443,12 +432,8 @@
             pltpu.VMEM((shards, 8, LANES), f32),
             pltpu.VMEM(((shards + SIDE) * MODES, LANES), f32),
             pltpu.VMEM((shards, 1, LANES), f32),
-            pltpu.VMEM((shards, 1, LANES), f32),
             pltpu.VMEM((8, LANES), f32),
-            pltpu.VMEM((groups, 8, LANES), f32),
             pltpu.VMEM((blocks, length, LANES), f32),
-            pltpu.VMEM((2 * MODES, channels), f32),
-            pltpu.VMEM((8, LANES), f32),
             pltpu.SemaphoreType.DMA((5,)),
             pltpu.SemaphoreType.DMA((3,)),
             pltpu.SemaphoreType.DMA((2,)),
@@ -469,11 +454,11 @@
             jax.ShapeDtypeStruct((MODES, GROUP), f32),
             jax.ShapeDtypeStruct((GROUP,), f32),
         ],
-        in_specs=[vmem] * 3,
+        in_specs=[vmem] * 5,
         out_specs=[vmem] * 4,
         compiler_params=pltpu.CompilerParams(vmem_limit_bytes=60 * 1024 * 1024),
         name="finish",
-    )(grads, carry, totals)
+    )(grads, carry, totals, decay, residue)
     return out[None], grad_residue, grad_decay, grad_skip
 
 

time: 25.2 us -> 24.2 us (0.960)
  Pallas kernels: 24.5 us -> 23.4 us
    pallas_call x1, Pallas kernels: 22.6 us -> 21.5 us  [body(): pl.pallas_call(functools.partial(exchange_kernel, shards, groups, positio...]
where the time goes in v4:
time: 24.2 us; the launch traced here: 24.1 us
  Pallas kernels  23.4 us (97%)
  between operations  0.64 us (3%)
    pallas_call x1, Pallas kernels, body(): pl.pallas_call(functools.partial(exchange_kernel, shards, groups, positio...  21.5 us
    pallas_call x1, Pallas kernels, body(): pl.pallas_call(finish_kernel, out_shape=[jax.ShapeDtypeStruct((length, ch...  1.96 us

profile of v4, /device:TPU:1, one launch (start us, length us, event | category | flops | bytes accessed | tf_op | source)
XLA Modules:
  0.0 24.1 jit_solution(2961604043985830925)
XLA Ops:
  0.6 21.5 %exchange.1 = (f32[4,128,128]{2,1,0:T(8,128)}, f32[32,1,128]{2,1,0:T(1,128)}, f32[8,8,128]{2,1,0:T(8,128)}) custom-call(bf16[128,512]{1,0:T(8,128)(2,1)} %bitcast.4, bf16[128,512]{1,0:T(8,128)(2,1)} %bitcast.5, f32[8,512]{1,0:T(8,128)} %rates.1, f32[8,512]{1,0:T(8,128)} %residue.1, f32[1,512]{1,0:T(1,128)} %bitcast.6), custom_call_target="tpu_custom_call" | custom-call | tf_op jit(solution)/shard_map/exchange/pallas_call | solution.py:410
  22.1 2.0 %finish.1 = (f32[128,512]{1,0:T(8,128)}, f32[8,16]{1,0:T(8,128)}, f32[8,16]{1,0:T(8,128)}, f32[16]{0:T(128)}) custom-call(f32[4,128,128]{2,1,0:T(8,128)} %get-tuple-element.11.grads, f32[32,1,128]{2,1,0:T(1,128)} %get-tuple-element.12.zrx, f32[8,8,128]{2,1,0:T(8,128)} %get-tuple-element.13.prx, f32[8,512]{1,0:T(8,128)} %rates.1, f32[8,512]{1,0:T(8,128)} %residue.1), custom_call_target="tpu_custom_call" | custom-call | tf_op jit(solution)/shard_map/finish/pallas_call | solution.py:449

commit v5 on v4

--- a/solution.py
+++ b/solution.py
@@ -38,7 +38,7 @@
     return blocks
 
 
-def summarise(g, xs, cs, rates, factors, sums, lags, starts, tx):
+def run_sums(g, xs, cs, factors, sums, lags):
     lanes = pl.ds(pl.multiple_of(g * LANES, LANES), LANES)
     x = [xs[g, pl.ds(i, RUNS, stride=RUN), :] for i in range(RUN)]
     c = [cs[g, pl.ds(i, RUNS, stride=RUN), :] for i in range(RUN)]
@@ -53,48 +53,58 @@
             head = factor * (head + adjoint)
             adjoint = factor * adjoint + c[i]
         rows = pl.ds(mode * RUNS, RUNS)
-        sums[0, rows, :] = state
-        sums[1, rows, :] = tail
-        sums[2, rows, :] = adjoint
-        sums[3, rows, :] = head + adjoint
+        sums[g, 0, rows, :] = state
+        sums[g, 1, rows, :] = tail
+        sums[g, 2, rows, :] = adjoint
+        sums[g, 3, rows, :] = head + adjoint
     for lag in range(RUN):
         total = c[lag] * x[0]
         for i in range(1, RUN - lag):
             total = total + c[i + lag] * x[i]
-        lags[pl.ds(lag, 1), :] = jnp.sum(total, axis=0, keepdims=True)
-    rate = rates[:, lanes]
-    factor = factors[:, lanes]
+        lags[pl.ds(lag, 1), lanes] = jnp.sum(total, axis=0, keepdims=True)
+
+
+def join_runs(rates, factors, sums, lags, starts, tx):
+    blocks = sums.shape[0]
+    rate = rates[...]
+    factor = factors[...]
     power = jnp.exp(rate * -float(RUN))
 
     def spread(lag):
-        return jnp.broadcast_to(lags[pl.ds(lag, 1), :], (MODES, LANES))
-
-    zeros = jnp.zeros((MODES, LANES), jnp.float32)
+        return jnp.broadcast_to(lags[pl.ds(lag, 1), :], rate.shape)
+
+    def run(q, a):
+        parts = [sums[g, q, pl.ds(a, MODES, stride=RUNS), :] for g in range(blocks)]
+        return jnp.concatenate(parts, axis=1)
+
+    zeros = jnp.zeros(rate.shape, jnp.float32)
     inner, cross = spread(RUN - 1), zeros
     for lag in range(RUN - 2, -1, -1):
         cross = factor * cross + inner
         inner = factor * inner + spread(lag)
-    run = [[sums[q, pl.ds(a, MODES, stride=RUNS), :] for q in range(4)] for a in range(RUNS)]
     state, tail, outer = zeros, zeros, zeros
     befores = []
     for a in range(RUNS):
-        run_state, run_tail, run_adjoint, run_head = run[a]
         befores.append(state)
-        outer = outer + state * run_adjoint
-        cross = cross + state * run_head
-        tail = run_tail + power * (tail + float(RUN) * state)
-        state = run_state + power * state
-    adjoint, head = zeros, zeros
+        outer = outer + state * run(2, a)
+        cross = cross + state * run(3, a)
+        tail = run(1, a) + power * (tail + float(RUN) * state)
+        state = run(0, a) + power * state
+    adjoint, head, both = zeros, zeros, zeros
     for a in range(RUNS - 1, -1, -1):
-        run_state, run_tail, run_adjoint, run_head = run[a]
-        starts[g, pl.ds(a * MODES, MODES), :] = adjoint
-        cross = cross + adjoint * (run_tail + (float(RUN) * power) * befores[a])
-        head = run_head + power * (head + float(RUN) * adjoint)
-        adjoint = run_adjoint + power * adjoint
+        for g in range(blocks):
+            starts[g, pl.ds(a * MODES, MODES), :] = adjoint[:, g * LANES : (g + 1) * LANES]
+        cross = cross + adjoint * run(1, a)
+        both = both + adjoint * befores[a]
+        head = run(3, a) + power * (head + float(RUN) * adjoint)
+        adjoint = run(2, a) + power * adjoint
     inner = inner + factor * outer
-    tiles = swap_blocks([adjoint, state, head, state, inner, cross, spread(0), tail])
-    for i in range(SIDE):
-        tx[g * SIDE + i] = tiles[i]
+    cross = cross + (float(RUN) * power) * both
+    wide = [adjoint, state, head, state, inner, cross, spread(0), tail]
+    for g in range(blocks):
+        tiles = swap_blocks([value[:, g * LANES : (g + 1) * LANES] for value in wide])
+        for i in range(SIDE):
+            tx[g * SIDE + i] = tiles[i]
 
 
 def local_grads(g, cs, factors, residue, skip, starts, grads):
@@ -123,27 +133,31 @@
     return value
 
 
-def owner_sums(place, block, length, positions, rates, residue, rx, zbuf):
+def owner_factors(place, block, length, rates, residue):
     lanes = pl.ds(pl.multiple_of(block * LANES, LANES), LANES)
     rate = own_lanes(rates[:, lanes], place)
     weight = own_lanes(residue[:, lanes], place)
     factor = jnp.exp(-rate)
-    power = jnp.exp(rate * -float(length))
+    return factor, jnp.exp(rate * -float(length)), weight
+
+
+def owner_sums(factor, power, weight, length, positions, rx, zbuf):
     shards = rx.shape[0]
     zeros = jnp.zeros((MODES, LANES), jnp.float32)
     state, plain, by_state, by_adjoint, both = zeros, zeros, zeros, zeros, zeros
-    befores = []
+    befores, moved = [], []
     for k in range(shards):
         tile = rx[k]
         befores.append(state)
+        moved.append(roll(tile, 1))
         plain = plain + tile
-        by_state = by_state + state * roll(tile, 1)
+        by_state = by_state + state * moved[k]
         state = power * state + tile
     adjoint = zeros
     for k in range(shards - 1, -1, -1):
         tile = rx[k]
         zbuf[pl.ds(k * MODES, MODES), :] = adjoint
-        by_adjoint = by_adjoint + adjoint * roll(tile, 1)
+        by_adjoint = by_adjoint + adjoint * moved[k]
         both = both + befores[k] * roll(adjoint, 1)
         adjoint = power * adjoint + tile
     scale = 1.0 / positions
@@ -262,7 +276,9 @@
 
     @pl.loop(0, blocks)
     def _(g):
-        summarise(g, xs, cs, rates, factors, sums, lags, starts, tx)
+        run_sums(g, xs, cs, factors, sums, lags)
+
+    join_runs(rates, factors, sums, lags, starts, tx)
 
     rx[ctx] = tx[owned]
     pl.semaphore_wait(barrier, shards - 1 + half - 1 + late * 2 * half)
@@ -293,8 +309,9 @@
     store = pltpu.make_async_copy(grads, grads_out, out_sems.at[0])
     store.start()
     most = pl.ds(0, shards - 1)
+    factor, power, weight = owner_factors(lax.rem(owned, SIDE), owned // SIDE, length, rates, residue)
     pltpu.make_async_copy(rx.at[most], rx.at[most], ctx_sems.at[1]).wait()
-    owner_sums(lax.rem(owned, SIDE), owned // SIDE, length, positions, rates, residue, rx, zbuf)
+    owner_sums(factor, power, weight, length, positions, rx, zbuf)
     ptx[...] = pack_rows(zbuf, shards // SIDE)
 
     def send_totals(group):
@@ -425,8 +442,8 @@
             pltpu.VMEM((blocks, length, LANES), f32),
             pltpu.VMEM((blocks, length, LANES), f32),
             pltpu.VMEM((MODES, channels), f32),
-            pltpu.VMEM((4, MODES * RUNS, LANES), f32),
-            pltpu.VMEM((RUN, LANES), f32),
+            pltpu.VMEM((blocks, 4, MODES * RUNS, LANES), f32),
+            pltpu.VMEM((RUN, channels), f32),
             pltpu.VMEM((blocks, RUNS * MODES, LANES), f32),
             pltpu.VMEM((shards, 8, LANES), f32),
             pltpu.VMEM((shards, 8, LANES), f32),

time: 24.2 us -> 23.6 us (0.975)
  Pallas kernels: 23.4 us -> 22.8 us
    pallas_call x1, Pallas kernels: 21.5 us -> 20.9 us  [body(): pl.pallas_call(functools.partial(exchange_kernel, shards, groups, positio...]
where the time goes in v5:
time: 23.6 us; the launch traced here: 23.5 us
  Pallas kernels  22.8 us (97%)
  between operations  0.64 us (3%)
    pallas_call x1, Pallas kernels, body(): pl.pallas_call(functools.partial(exchange_kernel, shards, groups, positio...  20.9 us
    pallas_call x1, Pallas kernels, body(): pl.pallas_call(finish_kernel, out_shape=[jax.ShapeDtypeStruct((length, ch...  1.96 us

profile of v5, /device:TPU:1, one launch (start us, length us, event | category | flops | bytes accessed | tf_op | source)
XLA Modules:
  0.0 23.5 jit_solution(15057169380776273495)
XLA Ops:
  0.6 20.9 %exchange.1 = (f32[4,128,128]{2,1,0:T(8,128)}, f32[32,1,128]{2,1,0:T(1,128)}, f32[8,8,128]{2,1,0:T(8,128)}) custom-call(bf16[128,512]{1,0:T(8,128)(2,1)} %bitcast.4, bf16[128,512]{1,0:T(8,128)(2,1)} %bitcast.5, f32[8,512]{1,0:T(8,128)} %rates.1, f32[8,512]{1,0:T(8,128)} %residue.1, f32[1,512]{1,0:T(1,128)} %bitcast.6), custom_call_target="tpu_custom_call" | custom-call | tf_op jit(solution)/shard_map/exchange/pallas_call | solution.py:427
  21.5 2.0 %finish.1 = (f32[128,512]{1,0:T(8,128)}, f32[8,16]{1,0:T(8,128)}, f32[8,16]{1,0:T(8,128)}, f32[16]{0:T(128)}) custom-call(f32[4,128,128]{2,1,0:T(8,128)} %get-tuple-element.11.grads, f32[32,1,128]{2,1,0:T(1,128)} %get-tuple-element.12.zrx, f32[8,8,128]{2,1,0:T(8,128)} %get-tuple-element.13.prx, f32[8,512]{1,0:T(8,128)} %rates.1, f32[8,512]{1,0:T(8,128)} %residue.1), custom_call_target="tpu_custom_call" | custom-call | tf_op jit(solution)/shard_map/finish/pallas_call | solution.py:466

commit v6 on v5

--- a/solution.py
+++ b/solution.py
@@ -274,33 +274,41 @@
         for g in range(blocks):
             wide[g] = raw[:, pl.ds(g * LANES, LANES)].astype(jnp.float32)
 
+    def send_plane(plane):
+        @pl.loop(0, PLANE)
+        def _(d):
+            inside = lax.rem(ctx + d, PLANE)
+            part = plane * PLANE + inside
+            across = (shards // PLANE - 1 - plane) * PLANE + inside
+            peer = part + late * (across - part)
+
+            @pl.when(peer != ctx)
+            def _():
+                pltpu.make_async_remote_copy(
+                    src_ref=tx.at[part],
+                    dst_ref=rx.at[ctx],
+                    send_sem=ctx_sems.at[0],
+                    recv_sem=ctx_sems.at[1],
+                    device_id=(dp, peer),
+                    device_id_type=MESH,
+                ).start()
+
     @pl.loop(0, blocks)
     def _(g):
         run_sums(g, xs, cs, factors, sums, lags)
 
     join_runs(rates, factors, sums, lags, starts, tx)
+    pl.semaphore_wait(barrier, shards - 1 + half - 1 + late * 2 * half)
+    for plane in range(shards // PLANE):
+        send_plane(plane)
 
     rx[ctx] = tx[owned]
-    pl.semaphore_wait(barrier, shards - 1 + half - 1 + late * 2 * half)
 
     @pl.when(late == 1)
     def _():
         @pl.loop(0, half)
         def _(d):
             pl.semaphore_signal(ready_sem, inc=1, device_id=(other_half(d), ctx), device_id_type=MESH)
-
-    @pl.loop(1, shards)
-    def _(d):
-        peer = lax.rem(ctx + d, shards)
-        across = (shards // PLANE - 1 - peer // PLANE) * PLANE + lax.rem(peer, PLANE)
-        pltpu.make_async_remote_copy(
-            src_ref=tx.at[peer + late * (across - peer)],
-            dst_ref=rx.at[ctx],
-            send_sem=ctx_sems.at[0],
-            recv_sem=ctx_sems.at[1],
-            device_id=(dp, peer),
-            device_id_type=MESH,
-        ).start()
 
     @pl.loop(0, blocks)
     def _(g):

time: 23.6 us -> 23.1 us (0.979)
  Pallas kernels: 22.8 us -> 22.3 us
    pallas_call x1, Pallas kernels: 20.9 us -> 20.4 us  [body(): pl.pallas_call(functools.partial(exchange_kernel, shards, groups, positio...]
where the time goes in v6:
time: 23.1 us; the launch traced here: 23 us
  Pallas kernels  22.3 us (97%)
  between operations  0.64 us (3%)
    pallas_call x1, Pallas kernels, body(): pl.pallas_call(functools.partial(exchange_kernel, shards, groups, positio...  20.4 us
    pallas_call x1, Pallas kernels, body(): pl.pallas_call(finish_kernel, out_shape=[jax.ShapeDtypeStruct((length, ch...  1.96 us

profile of v6, /device:TPU:1, one launch (start us, length us, event | category | flops | bytes accessed | tf_op | source)
XLA Modules:
  0.0 23.0 jit_solution(8784003433433997446)
XLA Ops:
  0.6 20.4 %exchange.1 = (f32[4,128,128]{2,1,0:T(8,128)}, f32[32,1,128]{2,1,0:T(1,128)}, f32[8,8,128]{2,1,0:T(8,128)}) custom-call(bf16[128,512]{1,0:T(8,128)(2,1)} %bitcast.4, bf16[128,512]{1,0:T(8,128)(2,1)} %bitcast.5, f32[8,512]{1,0:T(8,128)} %rates.1, f32[8,512]{1,0:T(8,128)} %residue.1, f32[1,512]{1,0:T(1,128)} %bitcast.6), custom_call_target="tpu_custom_call" | custom-call | tf_op jit(solution)/shard_map/exchange/pallas_call | solution.py:435
  21.0 2.0 %finish.1 = (f32[128,512]{1,0:T(8,128)}, f32[8,16]{1,0:T(8,128)}, f32[8,16]{1,0:T(8,128)}, f32[16]{0:T(128)}) custom-call(f32[4,128,128]{2,1,0:T(8,128)} %get-tuple-element.11.grads, f32[32,1,128]{2,1,0:T(1,128)} %get-tuple-element.12.zrx, f32[8,8,128]{2,1,0:T(8,128)} %get-tuple-element.13.prx, f32[8,512]{1,0:T(8,128)} %rates.1, f32[8,512]{1,0:T(8,128)} %residue.1), custom_call_target="tpu_custom_call" | custom-call | tf_op jit(solution)/shard_map/finish/pallas_call | solution.py:474

commit v7 on v6

--- a/solution.py
+++ b/solution.py
@@ -14,6 +14,7 @@
 RUNS = 8
 RUN = 16
 SIDE = 8
+SENT = 7
 PLANE = 8
 
 
@@ -64,7 +65,7 @@
         lags[pl.ds(lag, 1), lanes] = jnp.sum(total, axis=0, keepdims=True)
 
 
-def join_runs(rates, factors, sums, lags, starts, tx):
+def join_runs(rates, factors, sums, lags, starts, stage, tx):
     blocks = sums.shape[0]
     rate = rates[...]
     factor = factors[...]
@@ -100,9 +101,12 @@
         adjoint = run(2, a) + power * adjoint
     inner = inner + factor * outer
     cross = cross + (float(RUN) * power) * both
-    wide = [adjoint, state, head, state, inner, cross, spread(0), tail]
+    wide = [tail, adjoint, state, head, inner, cross, spread(0), zeros]
     for g in range(blocks):
-        tiles = swap_blocks([value[:, g * LANES : (g + 1) * LANES] for value in wide])
+        for q in range(SIDE):
+            stage[g, pl.ds(q * MODES, MODES), :] = wide[q][:, g * LANES : (g + 1) * LANES]
+    for g in range(blocks):
+        tiles = swap_blocks([stage[g, pl.ds(m, SIDE, stride=MODES), :] for m in range(MODES)])
         for i in range(SIDE):
             tx[g * SIDE + i] = tiles[i]
 
@@ -133,49 +137,48 @@
     return value
 
 
+def own_row(value, place):
+    return jnp.sum(jnp.where(own_rows() == lane_group(), own_lanes(value, place), 0.0), axis=0, keepdims=True)
+
+
+def own_rows():
+    return lax.broadcasted_iota(jnp.int32, (8, LANES), 0)
+
+
 def owner_factors(place, block, length, rates, residue):
     lanes = pl.ds(pl.multiple_of(block * LANES, LANES), LANES)
-    rate = own_lanes(rates[:, lanes], place)
-    weight = own_lanes(residue[:, lanes], place)
-    factor = jnp.exp(-rate)
-    return factor, jnp.exp(rate * -float(length)), weight
-
-
-def owner_sums(factor, power, weight, length, positions, rx, zbuf):
+    rate = own_row(rates[:, lanes], place)
+    weight = own_row(residue[:, lanes], place)
+    return jnp.exp(-rate), jnp.exp(rate * -float(length)), weight
+
+
+def owner_sums(factor, power, weight, length, positions, rx, ztx, ptx):
     shards = rx.shape[0]
-    zeros = jnp.zeros((MODES, LANES), jnp.float32)
-    state, plain, by_state, by_adjoint, both = zeros, zeros, zeros, zeros, zeros
+    zeros = jnp.zeros((SIDE, LANES), jnp.float32)
+    step = jnp.broadcast_to(power, (SIDE, LANES))
+    state, plain, by_start, by_head, by_tail, both = zeros, zeros, zeros, zeros, zeros, zeros
     befores, moved = [], []
     for k in range(shards):
         tile = rx[k]
         befores.append(state)
-        moved.append(roll(tile, 1))
+        moved.append(pltpu.roll(tile, 1, 0))
         plain = plain + tile
-        by_state = by_state + state * moved[k]
-        state = power * state + tile
+        by_start = by_start + state * moved[k]
+        by_head = by_head + state * pltpu.roll(tile, SIDE - 1, 0)
+        state = step * state + tile
     adjoint = zeros
     for k in range(shards - 1, -1, -1):
-        tile = rx[k]
-        zbuf[pl.ds(k * MODES, MODES), :] = adjoint
-        by_adjoint = by_adjoint + adjoint * moved[k]
-        both = both + befores[k] * roll(adjoint, 1)
-        adjoint = power * adjoint + tile
+        ztx[k] = adjoint[1:2]
+        by_tail = by_tail + adjoint * moved[k]
+        both = both + befores[k] * pltpu.roll(adjoint, 1, 0)
+        adjoint = step * adjoint + rx[k]
     scale = 1.0 / positions
-    sum_residue = roll(plain, -4) + factor * roll(by_state, -1)
-    sum_decay = roll(plain, -5) + roll(by_state, -3) + by_adjoint + (float(length) * power) * roll(both, -1)
-    sum_skip = roll(plain, -6)
-    last = [sum_residue * scale, (-scale) * factor * weight * sum_decay, sum_skip * scale]
-    for k in range(SIDE):
-        zbuf[pl.ds((shards + k) * MODES, MODES), :] = last[k] if k < len(last) else zeros
-
-
-def pack_rows(zbuf, a):
-    group = lane_group()
-    packed = zbuf[pl.ds(a * SIDE * MODES, SIDE, stride=MODES), :]
-    for mode in range(1, MODES):
-        rows = zbuf[pl.ds(a * SIDE * MODES + mode, SIDE, stride=MODES), :]
-        packed = jnp.where(group == mode, roll(rows, mode), packed)
-    return packed
+    sum_residue = plain[4:5] + factor * by_start[2:3]
+    sum_decay = plain[5:6] + by_head[2:3] + by_tail[1:2] + (float(length) * power) * both[2:3]
+    ptx[0:1] = sum_residue * scale
+    ptx[1:2] = (-scale) * factor * weight * sum_decay
+    ptx[2:3] = plain[6:7] * scale
+    ptx[3:8] = jnp.zeros((SIDE - 3, LANES), jnp.float32)
 
 
 def unpack_rows(rows):
@@ -210,9 +213,9 @@
     sums,
     lags,
     starts,
+    stage,
     tx,
     rx,
-    zbuf,
     ztx,
     ptx,
     grads,
@@ -246,6 +249,8 @@
     def other_half(d):
         return (1 - late) * half + d
 
+    sent = pl.ds(0, SENT)
+    rx[...] = jnp.zeros(rx.shape, jnp.float32)
     barrier = pltpu.get_barrier_semaphore()
 
     def greet(group, peer):
@@ -285,8 +290,8 @@
             @pl.when(peer != ctx)
             def _():
                 pltpu.make_async_remote_copy(
-                    src_ref=tx.at[part],
-                    dst_ref=rx.at[ctx],
+                    src_ref=tx.at[part, sent],
+                    dst_ref=rx.at[ctx, sent],
                     send_sem=ctx_sems.at[0],
                     recv_sem=ctx_sems.at[1],
                     device_id=(dp, peer),
@@ -297,7 +302,7 @@
     def _(g):
         run_sums(g, xs, cs, factors, sums, lags)
 
-    join_runs(rates, factors, sums, lags, starts, tx)
+    join_runs(rates, factors, sums, lags, starts, stage, tx)
     pl.semaphore_wait(barrier, shards - 1 + half - 1 + late * 2 * half)
     for plane in range(shards // PLANE):
         send_plane(plane)
@@ -318,9 +323,8 @@
     store.start()
     most = pl.ds(0, shards - 1)
     factor, power, weight = owner_factors(lax.rem(owned, SIDE), owned // SIDE, length, rates, residue)
-    pltpu.make_async_copy(rx.at[most], rx.at[most], ctx_sems.at[1]).wait()
-    owner_sums(factor, power, weight, length, positions, rx, zbuf)
-    ptx[...] = pack_rows(zbuf, shards // SIDE)
+    pltpu.make_async_copy(rx.at[most, sent], rx.at[most, sent], ctx_sems.at[1]).wait()
+    owner_sums(factor, power, weight, length, positions, rx, ztx, ptx)
 
     def send_totals(group):
         pltpu.make_async_remote_copy(
@@ -344,8 +348,6 @@
     def _(d):
         send_totals(same_half(d))
 
-    for a in range(shards // SIDE):
-        ztx[pl.ds(a * SIDE, SIDE)] = pack_rows(zbuf, a).reshape(SIDE, 1, LANES)
 
     @pl.loop(1, shards)
     def _(d):
@@ -372,7 +374,7 @@
 
     keep_row = pltpu.make_async_copy(ztx.at[ctx], zrx.at[owned], out_sems.at[2])
     keep_row.start()
-    pltpu.make_async_copy(tx.at[most], tx.at[most], ctx_sems.at[0]).wait()
+    pltpu.make_async_copy(tx.at[most, sent], tx.at[most, sent], ctx_sems.at[0]).wait()
     store.wait()
     keep_row.wait()
     pltpu.make_async_copy(zrx.at[most], zrx.at[most], back_sems.at[1]).wait()
@@ -453,9 +455,9 @@
             pltpu.VMEM((blocks, 4, MODES * RUNS, LANES), f32),
             pltpu.VMEM((RUN, channels), f32),
             pltpu.VMEM((blocks, RUNS * MODES, LANES), f32),
+            pltpu.VMEM((blocks, SIDE * MODES, LANES), f32),
             pltpu.VMEM((shards, 8, LANES), f32),
             pltpu.VMEM((shards, 8, LANES), f32),
-            pltpu.VMEM(((shards + SIDE) * MODES, LANES), f32),
             pltpu.VMEM((shards, 1, LANES), f32),
             pltpu.VMEM((8, LANES), f32),
             pltpu.VMEM((blocks, length, LANES), f32),

time: 23.1 us -> 22.7 us (0.983)
  Pallas kernels: 22.3 us -> 22 us
    pallas_call x1, Pallas kernels: 20.4 us -> 20 us  [body(): pl.pallas_call(functools.partial(exchange_kernel, shards, groups, positio...]
where the time goes in v7:
time: 22.7 us; the launch traced here: 22.6 us
  Pallas kernels  22 us (97%)
  between operations  0.64 us (3%)
    pallas_call x1, Pallas kernels, body(): pl.pallas_call(functools.partial(exchange_kernel, shards, groups, positio...  20 us
    pallas_call x1, Pallas kernels, body(): pl.pallas_call(finish_kernel, out_shape=[jax.ShapeDtypeStruct((length, ch...  1.96 us

profile of v7, /device:TPU:1, one launch (start us, length us, event | category | flops | bytes accessed | tf_op | source)
XLA Modules:
  0.0 22.6 jit_solution(17366228495654754779)
XLA Ops:
  0.6 20.0 %exchange.1 = (f32[4,128,128]{2,1,0:T(8,128)}, f32[32,1,128]{2,1,0:T(1,128)}, f32[8,8,128]{2,1,0:T(8,128)}) custom-call(bf16[128,512]{1,0:T(8,128)(2,1)} %bitcast.4, bf16[128,512]{1,0:T(8,128)(2,1)} %bitcast.5, f32[8,512]{1,0:T(8,128)} %rates.1, f32[8,512]{1,0:T(8,128)} %residue.1, f32[1,512]{1,0:T(1,128)} %bitcast.6), custom_call_target="tpu_custom_call" | custom-call | tf_op jit(solution)/shard_map/exchange/pallas_call | solution.py:437
  20.7 2.0 %finish.1 = (f32[128,512]{1,0:T(8,128)}, f32[8,16]{1,0:T(8,128)}, f32[8,16]{1,0:T(8,128)}, f32[16]{0:T(128)}) custom-call(f32[4,128,128]{2,1,0:T(8,128)} %get-tuple-element.11.grads, f32[32,1,128]{2,1,0:T(1,128)} %get-tuple-element.12.zrx, f32[8,8,128]{2,1,0:T(8,128)} %get-tuple-element.13.prx, f32[8,512]{1,0:T(8,128)} %rates.1, f32[8,512]{1,0:T(8,128)} %residue.1), custom_call_target="tpu_custom_call" | custom-call | tf_op jit(solution)/shard_map/finish/pallas_call | solution.py:476

commit v8 on v7

--- a/solution.py
+++ b/solution.py
@@ -14,6 +14,7 @@
 RUNS = 8
 RUN = 16
 SIDE = 8
+KEPT = 3
 SENT = 7
 PLANE = 8
 
@@ -250,6 +251,7 @@
         return (1 - late) * half + d
 
     sent = pl.ds(0, SENT)
+    kept = pl.ds(0, KEPT)
     rx[...] = jnp.zeros(rx.shape, jnp.float32)
     barrier = pltpu.get_barrier_semaphore()
 
@@ -282,7 +284,7 @@
     def send_plane(plane):
         @pl.loop(0, PLANE)
         def _(d):
-            inside = lax.rem(ctx + d, PLANE)
+            inside = d
             part = plane * PLANE + inside
             across = (shards // PLANE - 1 - plane) * PLANE + inside
             peer = part + late * (across - part)
@@ -328,8 +330,8 @@
 
     def send_totals(group):
         pltpu.make_async_remote_copy(
-            src_ref=ptx,
-            dst_ref=prx.at[dp],
+            src_ref=ptx.at[kept],
+            dst_ref=prx.at[dp, kept],
             send_sem=dp_sems.at[0],
             recv_sem=dp_sems.at[1],
             device_id=(group, owned),
@@ -363,7 +365,7 @@
 
     @pl.when(late == 0)
     def _():
-        keep = pltpu.make_async_copy(ptx, prx.at[dp], out_sems.at[1])
+        keep = pltpu.make_async_copy(ptx.at[kept], prx.at[dp, kept], out_sems.at[1])
         keep.start()
         keep.wait()
         pl.semaphore_wait(ready_sem, half)
@@ -383,12 +385,12 @@
     def wait_totals(sem):
         @pl.when(late == 1)
         def _():
-            pltpu.make_async_copy(prx, prx, sem).wait()
+            pltpu.make_async_copy(prx.at[:, kept], prx.at[:, kept], sem).wait()
 
         @pl.when(late == 0)
         def _():
             others = pl.ds(0, groups - 1)
-            pltpu.make_async_copy(prx.at[others], prx.at[others], sem).wait()
+            pltpu.make_async_copy(prx.at[others, kept], prx.at[others, kept], sem).wait()
 
     wait_totals(dp_sems.at[1])
     wait_totals(dp_sems.at[0])

time: 22.7 us -> 22.5 us (level)
  no operation moved by 1% of the time
where the time goes in v8:
time: 22.5 us; the launch traced here: 22.4 us
  Pallas kernels  21.8 us (97%)
  between operations  0.64 us (3%)
    pallas_call x1, Pallas kernels, body(): pl.pallas_call(functools.partial(exchange_kernel, shards, groups, positio...  19.8 us
    pallas_call x1, Pallas kernels, body(): pl.pallas_call(finish_kernel, out_shape=[jax.ShapeDtypeStruct((length, ch...  1.96 us

profile of v8, /device:TPU:1, one launch (start us, length us, event | category | flops | bytes accessed | tf_op | source)
XLA Modules:
  0.0 22.4 jit_solution(4843974886883255683)
XLA Ops:
  0.6 19.8 %exchange.1 = (f32[4,128,128]{2,1,0:T(8,128)}, f32[32,1,128]{2,1,0:T(1,128)}, f32[8,8,128]{2,1,0:T(8,128)}) custom-call(bf16[128,512]{1,0:T(8,128)(2,1)} %bitcast.4, bf16[128,512]{1,0:T(8,128)(2,1)} %bitcast.5, f32[8,512]{1,0:T(8,128)} %rates.1, f32[8,512]{1,0:T(8,128)} %residue.1, f32[1,512]{1,0:T(1,128)} %bitcast.6), custom_call_target="tpu_custom_call" | custom-call | tf_op jit(solution)/shard_map/exchange/pallas_call | solution.py:439
  20.5 2.0 %finish.1 = (f32[128,512]{1,0:T(8,128)}, f32[8,16]{1,0:T(8,128)}, f32[8,16]{1,0:T(8,128)}, f32[16]{0:T(128)}) custom-call(f32[4,128,128]{2,1,0:T(8,128)} %get-tuple-element.11.grads, f32[32,1,128]{2,1,0:T(1,128)} %get-tuple-element.12.zrx, f32[8,8,128]{2,1,0:T(8,128)} %get-tuple-element.13.prx, f32[8,512]{1,0:T(8,128)} %rates.1, f32[8,512]{1,0:T(8,128)} %residue.1), custom_call_target="tpu_custom_call" | custom-call | tf_op jit(solution)/shard_map/finish/pallas_call | solution.py:478

commit v9 on v8

--- a/solution.py
+++ b/solution.py
@@ -258,17 +258,17 @@
     def greet(group, peer):
         pl.semaphore_signal(barrier, inc=1, device_id=(group, peer), device_id_type=MESH)
 
-    @pl.loop(1, shards)
+    @pl.loop(1, shards, unroll=True)
     def _(d):
         greet(dp, lax.rem(ctx + d, shards))
 
-    @pl.loop(1, half)
+    @pl.loop(1, half, unroll=True)
     def _(d):
         greet(same_half(d), owned)
 
     @pl.when(late == 0)
     def _():
-        @pl.loop(0, half)
+        @pl.loop(0, half, unroll=True)
         def _(d):
             greet(other_half(d), mirror)
             greet(other_half(d), ctx)
@@ -282,7 +282,7 @@
             wide[g] = raw[:, pl.ds(g * LANES, LANES)].astype(jnp.float32)
 
     def send_plane(plane):
-        @pl.loop(0, PLANE)
+        @pl.loop(0, PLANE, unroll=True)
         def _(d):
             inside = d
             part = plane * PLANE + inside
@@ -313,7 +313,7 @@
 
     @pl.when(late == 1)
     def _():
-        @pl.loop(0, half)
+        @pl.loop(0, half, unroll=True)
         def _(d):
             pl.semaphore_signal(ready_sem, inc=1, device_id=(other_half(d), ctx), device_id_type=MESH)
 
@@ -340,18 +340,18 @@
 
     @pl.when(late == 1)
     def _():
-        @pl.loop(0, half)
+        @pl.loop(0, half, unroll=True)
         def _(d):
             send_totals(other_half(d))
 
         send_totals(dp)
 
-    @pl.loop(1, half)
+    @pl.loop(1, half, unroll=True)
     def _(d):
         send_totals(same_half(d))
 
 
-    @pl.loop(1, shards)
+    @pl.loop(1, shards, unroll=True)
     def _(d):
         peer = lax.rem(ctx + d, shards)
         pltpu.make_async_remote_copy(
@@ -370,7 +370,7 @@
         keep.wait()
         pl.semaphore_wait(ready_sem, half)
 
-        @pl.loop(0, half)
+        @pl.loop(0, half, unroll=True)
         def _(d):
             send_totals(other_half(d))
 

time: 22.5 us -> 22.3 us (level)
  no operation moved by 1% of the time
where the time goes in v9:
time: 22.3 us; the launch traced here: 22.2 us
  Pallas kernels  21.6 us (97%)
  between operations  0.64 us (3%)
    pallas_call x1, Pallas kernels, body(): pl.pallas_call(functools.partial(exchange_kernel, shards, groups, positio...  19.6 us
    pallas_call x1, Pallas kernels, body(): pl.pallas_call(finish_kernel, out_shape=[jax.ShapeDtypeStruct((length, ch...  1.96 us

profile of v9, /device:TPU:1, one launch (start us, length us, event | category | flops | bytes accessed | tf_op | source)
XLA Modules:
  0.0 22.2 jit_solution(11130476497123546323)
XLA Ops:
  0.6 19.6 %exchange.1 = (f32[4,128,128]{2,1,0:T(8,128)}, f32[32,1,128]{2,1,0:T(1,128)}, f32[8,8,128]{2,1,0:T(8,128)}) custom-call(bf16[128,512]{1,0:T(8,128)(2,1)} %bitcast.4, bf16[128,512]{1,0:T(8,128)(2,1)} %bitcast.5, f32[8,512]{1,0:T(8,128)} %rates.1, f32[8,512]{1,0:T(8,128)} %residue.1, f32[1,512]{1,0:T(1,128)} %bitcast.6), custom_call_target="tpu_custom_call" | custom-call | tf_op jit(solution)/shard_map/exchange/pallas_call | solution.py:439
  20.3 2.0 %finish.1 = (f32[128,512]{1,0:T(8,128)}, f32[8,16]{1,0:T(8,128)}, f32[8,16]{1,0:T(8,128)}, f32[16]{0:T(128)}) custom-call(f32[4,128,128]{2,1,0:T(8,128)} %get-tuple-element.11.grads, f32[32,1,128]{2,1,0:T(1,128)} %get-tuple-element.12.zrx, f32[8,8,128]{2,1,0:T(8,128)} %get-tuple-element.13.prx, f32[8,512]{1,0:T(8,128)} %rates.1, f32[8,512]{1,0:T(8,128)} %residue.1), custom_call_target="tpu_custom_call" | custom-call | tf_op jit(solution)/shard_map/finish/pallas_call | solution.py:478

commit v10 on v9

--- a/solution.py
+++ b/solution.py
@@ -399,10 +399,13 @@
 def finish_kernel(grads, zrx, prx, rates, residue, out, out_residue, out_decay, out_skip):
     blocks, length, _ = grads.shape
     ahead = (SIDE - lax.broadcasted_iota(jnp.int32, (8, LANES), 0)).astype(jnp.float32)
+    powers = jnp.exp(rates[...] * -8.0)
     for g in range(blocks):
         lanes = pl.ds(g * LANES, LANES)
         rate = [jnp.broadcast_to(rates[pl.ds(m, 1), lanes], (8, LANES)) for m in range(MODES)]
-        power = [jnp.exp(rate[m] * -8.0) for m in range(MODES)]
+        power = [
+            jnp.broadcast_to(powers[m : m + 1, g * LANES : (g + 1) * LANES], (8, LANES)) for m in range(MODES)
+        ]
         start = residue[:, lanes] * unpack_rows(zrx[pl.ds(g * SIDE, SIDE)].reshape(SIDE, LANES))
         term = [
             jnp.exp(-rate[m] * ahead) * jnp.broadcast_to(start[m : m + 1], (8, LANES))

time: 22.3 us -> 22.3 us (level)
  no operation moved by 1% of the time
where the time goes in v10:
time: 22.3 us; the launch traced here: 22.2 us
  Pallas kernels  21.6 us (97%)
  between operations  0.64 us (3%)
    pallas_call x1, Pallas kernels, body(): pl.pallas_call(functools.partial(exchange_kernel, shards, groups, positio...  19.6 us
    pallas_call x1, Pallas kernels, body(): pl.pallas_call(finish_kernel, out_shape=[jax.ShapeDtypeStruct((length, ch...  1.96 us

profile of v10, /device:TPU:1, one launch (start us, length us, event | category | flops | bytes accessed | tf_op | source)
XLA Modules:
  0.0 22.2 jit_solution(8934651736131000724)
XLA Ops:
  0.6 19.6 %exchange.1 = (f32[4,128,128]{2,1,0:T(8,128)}, f32[32,1,128]{2,1,0:T(1,128)}, f32[8,8,128]{2,1,0:T(8,128)}) custom-call(bf16[128,512]{1,0:T(8,128)(2,1)} %bitcast.4, bf16[128,512]{1,0:T(8,128)(2,1)} %bitcast.5, f32[8,512]{1,0:T(8,128)} %rates.1, f32[8,512]{1,0:T(8,128)} %residue.1, f32[1,512]{1,0:T(1,128)} %bitcast.6), custom_call_target="tpu_custom_call" | custom-call | tf_op jit(solution)/shard_map/exchange/pallas_call | solution.py:442
  20.3 2.0 %finish.1 = (f32[128,512]{1,0:T(8,128)}, f32[8,16]{1,0:T(8,128)}, f32[8,16]{1,0:T(8,128)}, f32[16]{0:T(128)}) custom-call(f32[4,128,128]{2,1,0:T(8,128)} %get-tuple-element.11.grads, f32[32,1,128]{2,1,0:T(1,128)} %get-tuple-element.12.zrx, f32[8,8,128]{2,1,0:T(8,128)} %get-tuple-element.13.prx, f32[8,512]{1,0:T(8,128)} %rates.1, f32[8,512]{1,0:T(8,128)} %residue.1), custom_call_target="tpu_custom_call" | custom-call | tf_op jit(solution)/shard_map/finish/pallas_call | solution.py:481

commit v11 on v10

--- a/solution.py
+++ b/solution.py
@@ -236,8 +236,6 @@
             ((tokens, x_raw), (cotangent, c_raw), (rates_in, rates), (residue_in, residue), (skip_in, skip))
         )
     ]
-    for load in loads:
-        load.start()
     half = groups // 2
     late = dp // half
     place_x = lax.rem(dp, half)
@@ -261,6 +259,9 @@
     @pl.loop(1, shards, unroll=True)
     def _(d):
         greet(dp, lax.rem(ctx + d, shards))
+
+    for load in loads:
+        load.start()
 
     @pl.loop(1, half, unroll=True)
     def _(d):

time: 22.3 us -> 22.3 us (level)
  no operation moved by 1% of the time
where the time goes in v11:
time: 22.3 us; the launch traced here: 22.2 us
  Pallas kernels  21.6 us (97%)
  between operations  0.64 us (3%)
    pallas_call x1, Pallas kernels, body(): pl.pallas_call(functools.partial(exchange_kernel, shards, groups, positio...  19.6 us
    pallas_call x1, Pallas kernels, body(): pl.pallas_call(finish_kernel, out_shape=[jax.ShapeDtypeStruct((length, ch...  1.96 us

profile of v11, /device:TPU:1, one launch (start us, length us, event | category | flops | bytes accessed | tf_op | source)
XLA Modules:
  0.0 22.2 jit_solution(5374496947696015323)
XLA Ops:
  0.6 19.6 %exchange.1 = (f32[4,128,128]{2,1,0:T(8,128)}, f32[32,1,128]{2,1,0:T(1,128)}, f32[8,8,128]{2,1,0:T(8,128)}) custom-call(bf16[128,512]{1,0:T(8,128)(2,1)} %bitcast.4, bf16[128,512]{1,0:T(8,128)(2,1)} %bitcast.5, f32[8,512]{1,0:T(8,128)} %rates.1, f32[8,512]{1,0:T(8,128)} %residue.1, f32[1,512]{1,0:T(1,128)} %bitcast.6), custom_call_target="tpu_custom_call" | custom-call | tf_op jit(solution)/shard_map/exchange/pallas_call | solution.py:443
  20.3 2.0 %finish.1 = (f32[128,512]{1,0:T(8,128)}, f32[8,16]{1,0:T(8,128)}, f32[8,16]{1,0:T(8,128)}, f32[16]{0:T(128)}) custom-call(f32[4,128,128]{2,1,0:T(8,128)} %get-tuple-element.11.grads, f32[32,1,128]{2,1,0:T(1,128)} %get-tuple-element.12.zrx, f32[8,8,128]{2,1,0:T(8,128)} %get-tuple-element.13.prx, f32[8,512]{1,0:T(8,128)} %rates.1, f32[8,512]{1,0:T(8,128)} %residue.1), custom_call_target="tpu_custom_call" | custom-call | tf_op jit(solution)/shard_map/finish/pallas_call | solution.py:482
